TPU v7x, 256 devices: a whole 4x4x8 slice. The times are simulated.
256 devices in a mesh: prow: 32 (over z_hi, x, core), pcol: 8 (over z_lo, y).
Axes of the slice: x: 4, y: 4, z: 8 (z_hi: 4, z_lo: 2; z = z_hi * 2 + z_lo), core: 2. Of those that a mesh axis runs over, the one named last changes fastest.
Arguments:
- matrix: float32 [40960, 8192], P('prow', 'pcol'), may hold values from -6 to 6
- pivots: int32 [2, 256], replicated, may hold values from 0 to 40959, as said below
- lower_inverse: float32 [2, 256, 256], replicated, as said below
- upper_inverse: float32 [2, 256, 256], replicated, as said below
Outputs:
- factored: float32 [40960, 8192], P('prow', 'pcol')
Inputs may be any that keep to these rules, and one draw needn't show every extreme that they name: `pivots`: the 512 pivot indices are distinct over both steps and none lies in rows k * 1280 to k * 1280 + 255 for k = 0 or 1. `lower_inverse`: unit lower triangular. `upper_inverse`: upper triangular with positive diagonal.
All inputs are finite; a program needn't handle non-finite values.
Results may differ from a plain program's by a relative error of at most 0.0001.
Values sent between devices are 32-bit elements; how exact they have to be, the bound alone decides.
No kernel may reach another device: no remote copies, remote signals or barrier semaphores. Data moves between devices by JAX's collectives and lax.ppermute only.
A program may use at most 64 MiB of HBM per device.

v0:
```python
import jax
import jax.numpy as jnp
from jax import lax
from jax.sharding import PartitionSpec as P


def from_root(value, axis, root):
    mine = lax.axis_index(axis) == root
    return lax.psum(jnp.where(mine, value, jnp.zeros_like(value)), axis)


def on_device(matrix, pivots, lower_inverse, upper_inverse):
    rows_dev, cols_dev = matrix.shape
    width = lower_inverse.shape[1]
    prow_index = lax.axis_index("prow")
    pcol_index = lax.axis_index("pcol")
    row_ids = lax.broadcasted_iota(jnp.int32, (rows_dev,), 0)
    col_ids = lax.broadcasted_iota(jnp.int32, (cols_dev,), 0)
    current = matrix
    for step in range(2):
        targets = pivots[step]
        offset = prow_index * rows_dev
        owned = (targets >= offset) & (targets < offset + rows_dev)
        local_rows = jnp.where(owned, targets - offset, 0)
        picked = jnp.where(owned[:, None], current[local_rows], 0.0)
        old_top = current[:width]
        on_root_row = prow_index == step
        row_keep = jnp.logical_not((prow_index <= step) & (row_ids < width))
        col_keep = jnp.logical_not((pcol_index <= step) & (col_ids < width))
        displaced = from_root(old_top, "prow", step)
        new_top = lax.psum(picked, "prow")
        upper_full = jnp.dot(
            lower_inverse[step],
            new_top,
            precision=lax.Precision.HIGHEST,
            preferred_element_type=jnp.float32,
        )
        merged = jnp.where(col_keep[None, :], upper_full, new_top)
        swapped = current.at[jnp.where(owned, targets - offset, rows_dev)].set(
            displaced, mode="drop"
        )
        top_rows = jnp.where(on_root_row, merged, swapped[:width])
        swapped = swapped.at[:width].set(top_rows)
        panel = swapped[:, :width]
        factor = jnp.dot(
            panel,
            upper_inverse[step],
            precision=lax.Precision.HIGHEST,
            preferred_element_type=jnp.float32,
        )
        factor = jnp.where(row_keep[:, None], factor, 0.0)
        factor = from_root(factor, "pcol", step)
        upper = jnp.where(col_keep[None, :], merged, 0.0)
        updated = swapped - jnp.dot(
            factor, upper, precision=lax.Precision.HIGHEST, preferred_element_type=jnp.float32
        )
        on_root_col = pcol_index == step
        panel_new = jnp.where(on_root_col & row_keep[:, None], factor, updated[:, :width])
        current = updated.at[:, :width].set(panel_new)
    return current


def solution(mesh):
    in_specs = (P("prow", "pcol"), P(), P(), P())
    out_specs = P("prow", "pcol")
    return jax.shard_map(
        on_device, mesh=mesh, in_specs=in_specs, out_specs=out_specs, check_vma=False
    )
```

profile of v0, /device:TPU:4, one launch (start us, length us, event | category | flops | bytes accessed | tf_op | source)
XLA Modules:
  0.0 861.7 jit_solution(11055075091690117205)
XLA Ops:
  6.5 5.7 copy.51
  12.3 4.1 gather_fusion
  18.8 283.9 %all-reduce.13.cloned.1.call-done = (f32[256,1024]{0,1:T(8,128)}, f32[256,1024]{0,1:T(8,128)}) async-done(((f32[256,1024]{0,1:T(8,128)}, f32[256,1024]{0,1:T(8,128)}), (f32[256,1024]{0,1:T(8,128)}, f32[256,1024]{0,1:T(8,128)})) %all-reduce.13.cloned.1.call-update) | async-done | bytes 2097168 | tf_op jit(solution)/shard_map/psum | solution.py:9
  302.7 1.6 copy.18
  304.2 6.2 scatter_fusion
  310.4 6.0 copy.21
  316.5 3.3 fusion.9
  319.7 3.7 fusion.1
  324.2 92.5 %all-reduce.7.cloned.1.call-done = f32[1280,256]{0,1:T(8,128)} async-done(((f32[1280,256]{0,1:T(8,128)}), f32[1280,256]{0,1:T(8,128)}) %all-reduce.7.cloned.1.call-update) | async-done | bytes 1310736 | tf_op jit(solution)/shard_map/psum | solution.py:9
  416.8 8.9 %convolution_subtract_fusion.1 = f32[1280,1024]{0,1:T(8,128)} fusion(f32[1280,1024]{0,1:T(8,128)} %get-tuple-element.69, f32[1280,256]{0,1:T(8,128)} %all-reduce.7.cloned.1.call-done, f32[256,1024]{0,1:T(8,128)S(1)} %get-tuple-element.70, pred[1024]{0:T(1024)(128)(4,1)S(1)} %fusion.30), kind=kOutput, calls=%fused_computation.5 | convolution fusion | flops 4028104704 | bytes 12846080 | tf_op jit(solution)/shard_map/dot_general | solution.py:54
  425.7 3.2 fusion.4
  428.9 5.9 copy.24
  434.8 4.1 gather_fusion.1
  439.2 2.3 slice_select_fusion.1
  442.8 280.3 %all-reduce.11.cloned.1.call-done = (f32[256,1024]{0,1:T(8,128)}, f32[256,1024]{0,1:T(8,128)}) async-done(((f32[256,1024]{0,1:T(8,128)}, f32[256,1024]{0,1:T(8,128)}), (f32[256,1024]{0,1:T(8,128)}, f32[256,1024]{0,1:T(8,128)})) %all-reduce.11.cloned.1.call-update) | async-done | bytes 2097168 | tf_op jit(solution)/shard_map/psum | solution.py:9
  723.2 1.6 copy.25
  724.7 6.2 scatter_fusion.1
  730.9 6.0 copy.29
  736.9 3.2 fusion.8
  740.1 3.7 fusion
  743.8 93.3 %all-reduce.9.cloned.1.call-done = f32[1280,256]{0,1:T(8,128)} async-done(((f32[1280,256]{0,1:T(8,128)}), f32[1280,256]{0,1:T(8,128)}) %all-reduce.9.cloned.1.call-update) | async-done | bytes 1310736 | tf_op jit(solution)/shard_map/psum | solution.py:9
  837.1 9.0 %convolution_subtract_fusion = f32[1280,1024]{0,1:T(8,128)} fusion(f32[1280,1024]{0,1:T(8,128)} %get-tuple-element.71, f32[1280,256]{0,1:T(8,128)} %all-reduce.9.cloned.1.call-done, f32[256,1024]{0,1:T(8,128)S(1)} %get-tuple-element.72, pred[1024]{0:T(1024)(128)(4,1)S(1)} %fusion.31), kind=kOutput, calls=%fused_computation.4 | convolution fusion | flops 4028104704 | bytes 12846080 | tf_op jit(solution)/shard_map/dot_general | solution.py:54
  846.1 3.2 fusion.5
  849.3 5.9 copy.32
  (40 shorter events, 4.7 us)
Async XLA Ops:
  6.5 5.7 copy-start.6
  6.5 296.1 %all-reduce.13.cloned.1.call-start = ((), (), s32[]{:S(2)}) async-start(), calls=%async_computation.3 | async-start | bytes 4194304 | tf_op jit(solution)/shard_map/psum | solution.py:9
  12.3 4.5 slice-start
  18.7 398.1 %all-reduce.7.cloned.1.call-start = ((), (), s32[]{:S(2)}) async-start(), calls=%async_computation | async-start | bytes 2621440 | tf_op jit(solution)/shard_map/psum | solution.py:9
  310.4 6.0 copy-start.2
  310.4 6.0 copy-start.5
  310.4 9.3 %copy-start.4 = (f32[2,256,256]{2,1,0:T(8,128)S(1)}, f32[2,256,256]{2,1,0:T(8,128)}, u32[]{:S(2)}) copy-start(f32[2,256,256]{2,1,0:T(8,128)} %param.15) | copy-start | bytes 1572868
  323.5 399.7 %all-reduce.11.cloned.1.call-start = ((), (), s32[]{:S(2)}) async-start(), calls=%async_computation.2 | async-start | bytes 4194304 | tf_op jit(solution)/shard_map/psum | solution.py:9
  416.8 8.9 %copy-start = (f32[1280,256]{0,1:T(8,128)S(1)}, f32[1280,256]{0,1:T(8,128)}, u32[]{:S(2)}) copy-start(f32[1280,256]{0,1:T(8,128)} %all-reduce.7.cloned.1.call-done) | copy-start | bytes 3932164
  442.6 394.5 %all-reduce.9.cloned.1.call-start = ((), (), s32[]{:S(2)}) async-start(), calls=%async_computation.1 | async-start | bytes 2621440 | tf_op jit(solution)/shard_map/psum | solution.py:9
  730.9 6.0 copy-start.3
  837.1 9.0 %copy-start.1 = (f32[1280,256]{0,1:T(8,128)S(1)}, f32[1280,256]{0,1:T(8,128)}, u32[]{:S(2)}) copy-start(f32[1280,256]{0,1:T(8,128)} %all-reduce.9.cloned.1.call-done) | copy-start | bytes 3932164
Sparse Core Ops, SparseCore 0:
  18.8 283.7 all-reduce.12
  323.6 93.1 all-reduce.6
  442.7 280.4 all-reduce.10
  743.9 93.0 all-reduce.8
where the time goes:
time: 863 us; the launch traced here: 862 us
  waiting for transfers between devices  750 us (87%)
  local copies, waits for them, and re-layouts  54.2 us (6%)
  matrix products  31.9 us (4%)
  between operations  13.3 us (2%)
  other arithmetic  12 us (1%)
    psum x4, waiting for transfers between devices, from_root(): return lax.psum(jnp.where(mine, value, jnp.zeros_like(value)), axis)  750 us
    scatter x4, local copies, waits for them, and re-layouts, on_device(): current.at[jnp.where(owned, targets - offset, rows_dev)]  24.4 us
    dot_general x2, matrix products, on_device(): jnp.dot(factor, upper, precision=lax.Precision.HIGHEST, preferred_element...  18 us
  transfers between devices with their start and end apart: 4, of which 4 were waited for; matrix products, arithmetic and copies ran while one was open for 0% of the time, Pallas kernels for 0%

commit v1 on v0

v1 whole, which is shorter than its diff:
```python
import functools

import jax
import jax.numpy as jnp
from jax import lax
from jax.experimental import pallas as pl
from jax.experimental.pallas import tpu as pltpu
from jax.sharding import PartitionSpec as P

NB = 256
ROWS_DEV = 1280
COLS_DEV = 1024
XS = 4
ZS = 4
QUARTER = NB // XS
SUB = QUARTER // ZS
EXT = COLS_DEV + NB + COLS_DEV + 2 * NB
BLOCK = 256
VMEM_LIMIT = 50 * 1024 * 1024


def shift(core, x, z):
    pairs = []
    for index in range(2 * XS * ZS):
        c, xi, zi = index % 2, index // 2 % XS, index // (2 * XS)
        target = ((zi + z) % ZS * XS + (xi + x) % XS) * 2 + (c + core) % 2
        pairs.append((index, target))
    return pairs


def send(value, core=0, x=0, z=0):
    return lax.ppermute(value, "prow", shift(core, x, z))


def send_from(value, keep, core=0, x=0, z=0):
    pairs = [pair for pair in shift(core, x, z) if keep(pair[0] // 2 % XS, pair[0] // (2 * XS))]
    return lax.ppermute(value, "prow", pairs)


def pick_kernel(place, pivots, a_ref, mine, theirs, rows, sources, count):
    prow, x, z, core = place[0], place[1], place[2], place[3]
    offset = prow * ROWS_DEV
    mine[...] = jnp.zeros_like(mine)
    theirs[...] = jnp.zeros_like(theirs)
    count[0] = 0
    for step in range(2):
        own = core == step

        def body(i, carry):
            local = pivots[step, i] - offset

            @pl.when((local >= 0) & (local < ROWS_DEV))
            def _():
                quarter, sub, low = i // QUARTER, i // SUB % ZS, i % SUB
                dest = (quarter - x + XS) % XS * QUARTER + (sub - z + ZS) % ZS * SUB + low
                where = (x - quarter + XS) % XS * QUARTER + (z - sub + ZS) % ZS * SUB + low
                n = count[0]
                rows[n] = local
                sources[n] = where + jnp.where(own, 0, NB)
                count[0] = n + 1
                row = a_ref[pl.ds(local, 1), :]

                @pl.when(own)
                def _():
                    mine[pl.ds(dest, 1), :] = row

                @pl.when(jnp.logical_not(own))
                def _():
                    theirs[pl.ds(dest, 1), :] = row

            return carry

        lax.fori_loop(0, NB, body, 0, unroll=8)


def pick(place, pivots, matrix):
    smem = pl.BlockSpec(memory_space=pltpu.SMEM)
    vmem = pl.BlockSpec(memory_space=pltpu.VMEM)
    half = jax.ShapeDtypeStruct((NB, COLS_DEV), jnp.float32)
    entries = jax.ShapeDtypeStruct((2 * NB,), jnp.int32)
    return pl.pallas_call(
        pick_kernel,
        out_shape=[half, half, entries, entries, jax.ShapeDtypeStruct((1,), jnp.int32)],
        in_specs=[smem, smem, vmem],
        out_specs=[vmem, vmem, smem, smem, smem],
        compiler_params=pltpu.CompilerParams(vmem_limit_bytes=VMEM_LIMIT),
        name="pick_rows",
    )(place, pivots, matrix)


def split(value):
    high = value.astype(jnp.bfloat16)
    low = (value - high.astype(jnp.float32)).astype(jnp.bfloat16)
    return high, low


def mul(a, b):
    dot = functools.partial(jnp.dot, preferred_element_type=jnp.float32)
    return dot(a[0], b[0]) + (dot(a[0], b[1]) + dot(a[1], b[0]))


def update_kernel(
    place, rows, sources, count, a_ref, p_ref, g0_ref, g1_ref, m_ref, w_ref, out_ref,
    xs, uh, ul, top, ph, wh, wl, ch, cl,
):
    prow, x, z, core, pcol = place[0], place[1], place[2], place[3], place[4]
    block = pl.program_id(0)

    @pl.when(block == 0)
    def _():
        for part, g_ref in ((0, g0_ref), (1, g1_ref)):
            step = core if part == 0 else 1 - core
            for j in range(XS):
                for k in range(ZS):
                    dest = step * NB + (x - j + XS) % XS * QUARTER + (z - k + ZS) % ZS * SUB
                    dest = pl.multiple_of(dest, SUB)
                    src = j * QUARTER + k * SUB
                    xs[pl.ds(dest, SUB), :] = g_ref[src:src + SUB, : COLS_DEV + NB]
        w0, w1 = split(w_ref[0]), split(w_ref[1])
        wh[0], wl[0] = w0
        wh[1], wl[1] = w1
        m0, m1 = split(m_ref[0]), split(m_ref[1])
        l0r1 = mul(split(xs[NB:, COLS_DEV:]), w0)
        u0c1 = mul(m0, split(xs[:NB, COLS_DEV:]))
        ch[...], cl[...] = split(u0c1)
        l0r1s = split(l0r1)
        for n in range(COLS_DEV // NB):
            cols = slice(n * NB, (n + 1) * NB)
            x0 = xs[:NB, cols]
            u0 = mul(m0, split(x0))
            u0s = split(u0)
            y1 = xs[NB:, cols] - mul(l0r1s, u0s)
            u1 = mul(m1, split(y1))
            u1s = split(u1)
            uh[:NB, cols], ul[:NB, cols] = u0s
            uh[NB:, cols], ul[NB:, cols] = u1s
            if n == 0:
                u0 = jnp.where(pcol == 0, x0, u0)
                u1 = jnp.where(pcol == 0, l0r1, jnp.where(pcol == 1, y1, u1))
            top[:, cols] = jnp.where(prow == 0, u0, u1)

    @pl.when((block == 0) & (prow < 2))
    def _():
        out_ref[...] = top[...]

    @pl.when((block > 0) | (prow >= 2))
    def _():
        out_ref[...] = a_ref[...]
        ph[...] = p_ref[...]
        base = block * BLOCK

        def patch(n, carry):
            local = rows[n] - base

            @pl.when((local >= 0) & (local < BLOCK))
            def _():
                src = sources[n]

                @pl.when(src < NB)
                def _():
                    row = g0_ref[pl.ds(src, 1), COLS_DEV + NB:]
                    out_ref[pl.ds(local, 1), :] = row[:, :COLS_DEV]
                    ph[pl.ds(local, 1), :] = row[:, COLS_DEV:]

                @pl.when(src >= NB)
                def _():
                    row = g1_ref[pl.ds(src - NB, 1), COLS_DEV + NB:]
                    out_ref[pl.ds(local, 1), :] = row[:, :COLS_DEV]
                    ph[pl.ds(local, 1), :] = row[:, COLS_DEV:]

            return carry

        lax.fori_loop(0, count[0], patch, 0)
        w0, w1 = (wh[0], wl[0]), (wh[1], wl[1])
        l0 = mul(split(ph[:, :NB]), w0)
        l0s = split(l0)
        l1 = mul(split(ph[:, NB:] - mul(l0s, (ch[...], cl[...]))), w1)
        l1s = split(l1)
        ls = tuple(jnp.concatenate([a, b], axis=1) for a, b in zip(l0s, l1s))
        for n in range(COLS_DEV // NB):
            cols = slice(n * NB, (n + 1) * NB)
            out_ref[:, cols] = out_ref[:, cols] - mul(ls, (uh[:, cols], ul[:, cols]))

        @pl.when(pcol == 0)
        def _():
            out_ref[:, :NB] = l0

        @pl.when(pcol == 1)
        def _():
            out_ref[:, :NB] = l1


def update(place, rows, sources, count, matrix, panels, g0, g1, lower, upper):
    smem = pl.BlockSpec(memory_space=pltpu.SMEM)
    vmem = pl.BlockSpec(memory_space=pltpu.VMEM)
    f32, bf16 = jnp.float32, jnp.bfloat16
    return pl.pallas_call(
        update_kernel,
        grid=(ROWS_DEV // BLOCK,),
        out_shape=jax.ShapeDtypeStruct((ROWS_DEV, COLS_DEV), f32),
        in_specs=[
            smem, smem, smem, smem,
            pl.BlockSpec((BLOCK, COLS_DEV), lambda i: (i, 0)),
            pl.BlockSpec((BLOCK, 2 * NB), lambda i: (i, 0)),
            vmem, vmem, vmem, vmem,
        ],
        out_specs=pl.BlockSpec((BLOCK, COLS_DEV), lambda i: (i, 0)),
        scratch_shapes=[
            pltpu.VMEM((2 * NB, COLS_DEV + NB), f32),
            pltpu.VMEM((2 * NB, COLS_DEV), bf16),
            pltpu.VMEM((2 * NB, COLS_DEV), bf16),
            pltpu.VMEM((NB, COLS_DEV), f32),
            pltpu.VMEM((BLOCK, 2 * NB), f32),
            pltpu.VMEM((2, NB, NB), bf16),
            pltpu.VMEM((2, NB, NB), bf16),
            pltpu.VMEM((NB, NB), bf16),
            pltpu.VMEM((NB, NB), bf16),
        ],
        compiler_params=pltpu.CompilerParams(vmem_limit_bytes=VMEM_LIMIT),
        name="panel_update",
    )(place, rows, sources, count, matrix, panels, g0, g1, lower, upper)


def on_device(matrix, pivots, lower_inverse, upper_inverse):
    prow, pcol = lax.axis_index("prow"), lax.axis_index("pcol")
    core, x, z = prow % 2, prow // 2 % XS, prow // (2 * XS)
    place = jnp.stack([prow, x, z, core, pcol]).astype(jnp.int32)

    scattered = lax.all_to_all(matrix[:, :NB], "pcol", 0, 0, tiled=True)
    part = ROWS_DEV // 8
    panels = jnp.concatenate([scattered[:part], scattered[part:2 * part]], axis=1)
    panels = lax.all_gather(panels, "pcol", tiled=True)

    mine, theirs, rows, sources, count = pick(place, pivots, matrix)
    total = (mine + send(theirs, core=1)).reshape(XS, QUARTER, COLS_DEV)
    total = total[0] + sum(send(total[j], x=j) for j in range(1, XS))
    total = total.reshape(ZS, SUB, COLS_DEV)
    total = total[0] + sum(send(total[k], z=k) for k in range(1, ZS))

    top = matrix[:NB].reshape(XS, QUARTER, COLS_DEV)
    spread = sum(
        send_from(top[j], lambda xi, zi: xi == 0 and zi == 0, x=j) for j in range(1, XS)
    )
    quarter = jnp.where(x == 0, top[0], spread).reshape(ZS, SUB, COLS_DEV)
    spread = sum(send_from(quarter[k], lambda xi, zi: zi == 0, z=k) for k in range(1, ZS))
    displaced = jnp.where(z == 0, quarter[0], spread)

    extra = jnp.concatenate([total[:, :NB], displaced[:, :NB]], axis=0)
    extra = lax.all_to_all(jnp.tile(extra, (8, 1)), "pcol", 0, 0, tiled=True)
    from_0, from_1 = extra[:2 * SUB], extra[2 * SUB:4 * SUB]
    crossed = jnp.where(core == 0, from_1[:SUB], from_0[:SUB])
    held = jnp.concatenate([total, crossed, displaced, from_0[SUB:], from_1[SUB:]], axis=1)

    held = jnp.concatenate([held] + [send(held, z=k) for k in range(1, ZS)], axis=0)
    held = jnp.concatenate([held] + [send(held, x=j) for j in range(1, XS)], axis=0)
    other = send(held, core=1)
    return update(
        place, rows, sources, count, matrix, panels, held, other, lower_inverse, upper_inverse
    )


def solution(mesh):
    in_specs = (P("prow", "pcol"), P(), P(), P())
    out_specs = P("prow", "pcol")
    return jax.shard_map(
        on_device, mesh=mesh, in_specs=in_specs, out_specs=out_specs, check_vma=False
    )
```

time: 863 us -> 185 us (0.21)
  waiting for transfers between devices: 750 us -> 80.9 us
  starting transfers between devices: 0.31 us -> 40.5 us
  local copies, waits for them, and re-layouts: 54.2 us -> 18.1 us
  matrix products: 31.9 us -> 0 us
  Pallas kernels: 0 us -> 28.4 us
  other arithmetic: 12 us -> 2.85 us
    psum x4 -> x0, waiting for transfers between devices: 750 us -> none  [from_root(): return lax.psum(jnp.where(mine, value, jnp.zeros_like(value)), axis)]
    ppermute x0 -> x20, waiting for transfers between devices: none -> 65.1 us  [the longest x14 62.2 us: send(): return lax.ppermute(value, 'prow', shift(core, x, z))]
    scatter x6 -> x0, local copies, waits for them, and re-layouts: 36.2 us -> none  [the longest x4 24.4 us: on_device(): current.at[jnp.where(owned, targets - offset, rows_dev)]]
    dot_general x6 -> x0, matrix products: 31.9 us -> none  [the longest x2 18 us: on_device(): jnp.dot(factor, upper, precision=lax.Precision.HIGHEST, preferred_element...]
    ppermute x0 -> x20, starting transfers between devices: none -> 31.5 us  [the longest x14 21.9 us: send(): return lax.ppermute(value, 'prow', shift(core, x, z))]
    pallas_call x0 -> x2, Pallas kernels: none -> 28.4 us  [the longest x1 18.2 us: update(): pl.pallas_call(update_kernel, grid=(ROWS_DEV // BLOCK,), out_shape=jax.Sh...]
    all_gather x0 -> x1, waiting for transfers between devices: none -> 11 us  [on_device(): panels = lax.all_gather(panels, 'pcol', tiled=True)]
    all_to_all x0 -> x2, starting transfers between devices: none -> 8.98 us  [the longest x1 5.41 us: on_device(): extra = lax.all_to_all(jnp.tile(extra, (8, 1)), 'pcol', 0, 0, tiled=True)]
  transfers between devices with their start and end apart: 4 -> 23, of which waited for: 4 -> 11; matrix products, arithmetic and copies ran while one was open for 0% -> 10% of each run, Pallas kernels for 0% -> 0%
where the time goes in v1:
time: 185 us; the launch traced here: 184 us
  waiting for transfers between devices  80.9 us (44%)
  starting transfers between devices  40.5 us (22%)
  Pallas kernels  28.4 us (15%)
  local copies, waits for them, and re-layouts  18.1 us (10%)
  between operations  13.6 us (7%)
  other arithmetic  2.85 us (2%)
    ppermute x14, waiting for transfers between devices, send(): return lax.ppermute(value, 'prow', shift(core, x, z))  62.2 us
    ppermute x14, starting transfers between devices, send(): return lax.ppermute(value, 'prow', shift(core, x, z))  21.9 us
    pallas_call x1, Pallas kernels, update(): pl.pallas_call(update_kernel, grid=(ROWS_DEV // BLOCK,), out_shape=jax.Sh...  18.2 us
    unnamed x23, local copies, waits for them, and re-layouts  11.8 us
    all_gather x1, waiting for transfers between devices, on_device(): panels = lax.all_gather(panels, 'pcol', tiled=True)  11 us
    pallas_call x1, Pallas kernels, pick(): pl.pallas_call(pick_kernel, out_shape=[half, half, entries, entries, jax....  10.2 us
    ppermute x6, starting transfers between devices, send_from(): return lax.ppermute(value, 'prow', pairs)  9.58 us
    all_to_all x1, starting transfers between devices, on_device(): extra = lax.all_to_all(jnp.tile(extra, (8, 1)), 'pcol', 0, 0, tiled=True)  5.41 us
  transfers between devices with their start and end apart: 23, of which 11 were waited for; matrix products, arithmetic and copies ran while one was open for 10% of the time, Pallas kernels for 0%

profile of v1, /device:TPU:4, one launch (start us, length us, event | category | flops | bytes accessed | tf_op | source)
XLA Modules:
  0.0 184.4 jit_solution(15405549708414667687)
XLA Ops:
  7.3 10.2 %pick_rows.1 = (f32[256,1024]{1,0:T(8,128)S(1)}, f32[256,1024]{1,0:T(8,128)S(1)}, s32[512]{0:T(512)S(1)}, s32[512]{0:T(512)S(1)}, s32[1]{0:T(128)}) custom-call(s32[5]{0:T(128)S(1)} %stack.23.place, s32[2,256]{1,0:T(2,128)S(1)} %copy-done.3, f32[1280,1024]{1,0:T(8,128)} %a_ref.3), custom_call_target="tpu_custom_call" | custom-call | tf_op jit(solution)/shard_map/pick_rows/pallas_call | solution.py:81
  17.6 2.0 %fusion = (f32[64,1024]{1,0:T(8,128)}, f32[64,1024]{1,0:T(8,128)}, f32[64,1024]{1,0:T(8,128)}) fusion(f32[1280,1024]{1,0:T(8,128)} %a_ref.3), kind=kLoop, calls=%fused_computation.26 | loop fusion | bytes 1572864 | tf_op jit(solution)/shard_map/slice | solution.py:242
  23.9 5.5 %collective-permute-start.2 = (f32[64,1024]{1,0:T(8,128)S(1)}, f32[64,1024]{1,0:T(8,128)S(1)}, u32[]{:S(2)}, u32[]{:S(2)}) collective-permute-start(f32[64,1024]{1,0:T(8,128)S(1)} %get-tuple-element.22), channel_id=1, source_target_pairs={{0,32},{8,40},{16,48},{24,56},{32,0},{40,8},{48,16},{56,24},{64,96... | collective-permute-start | bytes 786440 | tf_op jit(solution)/shard_map/ppermute | solution.py:32
  29.4 2.9 %collective-permute-done.8 = f32[64,1024]{1,0:T(8,128)S(1)} collective-permute-done((f32[64,1024]{1,0:T(8,128)}, f32[64,1024]{1,0:T(8,128)S(1)}, u32[]{:S(2)}, u32[]{:S(2)}) %collective-permute-start.8) | collective-permute-done | bytes 262176 | tf_op jit(solution)/shard_map/ppermute | solution.py:37
  33.5 3.0 %collective-permute-start.11 = (f32[16,1024]{1,0:T(8,128)S(1)}, f32[16,1024]{1,0:T(8,128)S(1)}, u32[]{:S(2)}, u32[]{:S(2)}) collective-permute-start(f32[16,1024]{1,0:T(8,128)S(1)} %get-tuple-element.27), channel_id=1, source_target_pairs={{0,128},{8,136},{16,144},{24,152},{32,160},{40,168},{48,176},{56,1... | collective-permute-start | bytes 196616 | tf_op jit(solution)/shard_map/ppermute | solution.py:37
  37.8 5.8 %collective-permute-done.2 = f32[64,1024]{1,0:T(8,128)S(1)} collective-permute-done((f32[64,1024]{1,0:T(8,128)S(1)}, f32[64,1024]{1,0:T(8,128)S(1)}, u32[]{:S(2)}, u32[]{:S(2)}) %collective-permute-start.2) | collective-permute-done | bytes 262176 | tf_op jit(solution)/shard_map/ppermute | solution.py:32
  46.5 2.9 %collective-permute-start.4 = (f32[16,1024]{1,0:T(8,128)S(1)}, f32[16,1024]{1,0:T(8,128)S(1)}, u32[]{:S(2)}, u32[]{:S(2)}) collective-permute-start(f32[16,1024]{1,0:T(8,128)S(1)} %get-tuple-element.32), channel_id=1, source_target_pairs={{0,64},{8,72},{16,80},{24,88},{32,96},{40,104},{48,112},{56,120},{... | collective-permute-start | bytes 196616 | tf_op jit(solution)/shard_map/ppermute | solution.py:32
  49.5 5.4 %collective-permute-done.5 = f32[16,1024]{1,0:T(8,128)S(1)} collective-permute-done((f32[16,1024]{1,0:T(8,128)S(1)}, f32[16,1024]{1,0:T(8,128)S(1)}, u32[]{:S(2)}, u32[]{:S(2)}) %collective-permute-start.5) | collective-permute-done | bytes 65568 | tf_op jit(solution)/shard_map/ppermute | solution.py:32
  56.4 5.4 %all-to-all-start.1 = ((f32[8,32,256]{2,1,0:T(8,128)}), f32[8,32,256]{2,1,0:T(8,128)S(1)}, u32[]{:S(2)}, u32[]{:S(2)}) async-start(f32[8,32,256]{2,1,0:T(8,128)} %tile.2), calls=%async_computation.1 | async-start | bytes 524288 | tf_op jit(solution)/shard_map/all_to_all | solution.py:249
  61.8 2.5 %slice.108 = f32[1280,256]{1,0:T(8,128)} slice(f32[1280,1024]{1,0:T(8,128)} %a_ref.3), slice={[0:1280], [0:256]} | slice | bytes 2621440 | tf_op jit(solution)/shard_map/slice | solution.py:229
  64.2 4.8 %all-to-all-done.1 = f32[8,32,256]{2,1,0:T(8,128)S(1)} async-done(((f32[8,32,256]{2,1,0:T(8,128)}), f32[8,32,256]{2,1,0:T(8,128)S(1)}, u32[]{:S(2)}, u32[]{:S(2)}) %all-to-all-start.1) | async-done | bytes 262176 | tf_op jit(solution)/shard_map/all_to_all | solution.py:249
  69.0 3.6 %all-to-all-start = ((f32[8,160,256]{2,1,0:T(8,128)}), f32[8,160,256]{2,1,0:T(8,128)S(1)}, u32[]{:S(2)}, u32[]{:S(2)}) async-start(f32[8,160,256]{2,1,0:T(8,128)} %bitcast.5), calls=%async_computation | async-start | bytes 2621440 | tf_op jit(solution)/shard_map/all_to_all | solution.py:229
  73.9 2.5 %collective-permute-start.15 = (f32[16,2816]{1,0:T(8,128)S(1)}, f32[16,2816]{1,0:T(8,128)S(1)}, u32[]{:S(2)}, u32[]{:S(2)}) collective-permute-start(f32[16,2816]{1,0:T(8,128)S(1)} %get-tuple-element.25), channel_id=1, source_target_pairs={{0,192},{8,200},{16,208},{24,216},{32,224},{40,232},{48,240},{56,2... | collective-permute-start | bytes 540680 | tf_op jit(solution)/shard_map/ppermute | solution.py:32
  76.4 1.9 %collective-permute-start.14 = (f32[16,2816]{1,0:T(8,128)S(1)}, f32[16,2816]{1,0:T(8,128)S(1)}, u32[]{:S(2)}, u32[]{:S(2)}) collective-permute-start(f32[16,2816]{1,0:T(8,128)S(1)} %get-tuple-element.25), channel_id=1, source_target_pairs={{0,128},{8,136},{16,144},{24,152},{32,160},{40,168},{48,176},{56,1... | collective-permute-start | bytes 540680 | tf_op jit(solution)/shard_map/ppermute | solution.py:32
  78.3 1.8 collective-permute-start.13
  81.9 17.3 %collective-permute-done.14 = f32[16,2816]{1,0:T(8,128)S(1)} collective-permute-done((f32[16,2816]{1,0:T(8,128)S(1)}, f32[16,2816]{1,0:T(8,128)S(1)}, u32[]{:S(2)}, u32[]{:S(2)}) %collective-permute-start.14) | collective-permute-done | bytes 180256 | tf_op jit(solution)/shard_map/ppermute | solution.py:32
  99.3 2.8 %collective-permute-done.13 = f32[16,2816]{1,0:T(8,128)S(1)} collective-permute-done((f32[16,2816]{1,0:T(8,128)S(1)}, f32[16,2816]{1,0:T(8,128)S(1)}, u32[]{:S(2)}, u32[]{:S(2)}) %collective-permute-start.13) | collective-permute-done | bytes 180256 | tf_op jit(solution)/shard_map/ppermute | solution.py:32
  102.1 4.1 %collective-permute-start.18 = (f32[64,2816]{1,0:T(8,128)S(1)}, f32[64,2816]{1,0:T(8,128)S(1)}, u32[]{:S(2)}, u32[]{:S(2)}) collective-permute-start(f32[64,2816]{1,0:T(8,128)S(1)} %pad_maximum_fusion), channel_id=1, source_target_pairs={{0,48},{8,56},{16,0},{24,8},{32,16},{40,24},{48,32},{56,40},{64,11... | collective-permute-start | bytes 2162696 | tf_op jit(solution)/shard_map/ppermute | solution.py:32
  106.2 2.1 %collective-permute-start.16 = (f32[64,2816]{1,0:T(8,128)S(1)}, f32[64,2816]{1,0:T(8,128)}, u32[]{:S(2)}, u32[]{:S(2)}) collective-permute-start(f32[64,2816]{1,0:T(8,128)S(1)} %pad_maximum_fusion), channel_id=1, source_target_pairs={{0,16},{8,24},{16,32},{24,40},{32,48},{40,56},{48,0},{56,8},{64,80... | collective-permute-start | bytes 2162696 | tf_op jit(solution)/shard_map/ppermute | solution.py:32
  113.0 24.0 %collective-permute-done.16 = f32[64,2816]{1,0:T(8,128)} collective-permute-done((f32[64,2816]{1,0:T(8,128)S(1)}, f32[64,2816]{1,0:T(8,128)}, u32[]{:S(2)}, u32[]{:S(2)}) %collective-permute-start.16) | collective-permute-done | bytes 720928 | tf_op jit(solution)/shard_map/ppermute | solution.py:32
  137.1 2.0 %constant_dynamic-update-slice_fusion.7 = f32[256,2816]{1,0:T(8,128)} fusion(f32[256,2816]{1,0:T(8,128)} %constant_dynamic-update-slice_fusion.8, f32[64,2816]{1,0:T(8,128)} %collective-permute-done.16), kind=kLoop, calls=%fused_computation.15 | loop fusion | bytes 1441792
  141.0 5.6 %collective-permute-done.19.g1_ref = f32[256,2816]{1,0:T(8,128)} collective-permute-done((f32[256,2816]{1,0:T(8,128)}, f32[256,2816]{1,0:T(8,128)}, u32[]{:S(2)}, u32[]{:S(2)}) %collective-permute-start.19) | collective-permute-done | bytes 2883616 | tf_op jit(solution)/shard_map/ppermute | solution.py:32
  146.6 11.0 %all-gather.2.cloned.1.call-done.p_ref = f32[1280,512]{1,0:T(8,128)} async-done(((f32[160,512]{1,0:T(8,128)}), f32[1280,512]{1,0:T(8,128)}) %all-gather.2.cloned.1.call-update) | async-done | bytes 2621456 | tf_op jit(solution)/shard_map/all_gather | solution.py:232
  159.3 18.2 %panel_update.1 = f32[1280,1024]{1,0:T(8,128)} custom-call(s32[5]{0:T(128)S(1)} %stack.23.place, s32[512]{0:T(512)S(1)} %get-tuple-element.10.rows, s32[512]{0:T(512)S(1)} %get-tuple-element.11.sources, s32[1]{0:T(128)} %get-tuple-element.12.count, f32[1280,1024]{1,0:T(8,128)} %a_ref.3, f32[1280,512]{1,0:T(8,128)S(1)} %copy-done, ...), custom_call_target="tpu_custom_call" | custom-call | tf_op jit(solution)/shard_map/panel_update/pallas_call | solution.py:197
  (69 shorter events, 23.6 us)
Async XLA Ops:
  17.5 6.1 %collective-permute-start = (f32[256,1024]{1,0:T(8,128)S(1)}, f32[256,1024]{1,0:T(8,128)S(1)}, u32[]{:S(2)}, u32[]{:S(2)}) collective-permute-start(f32[256,1024]{1,0:T(8,128)S(1)} %get-tuple-element.14), channel_id=1, source_target_pairs={{0,8},{8,0},{16,24},{24,16},{32,40},{40,32},{48,56},{56,48},{64,72... | collective-permute-start | bytes 3145736 | tf_op jit(solution)/shard_map/ppermute | solution.py:32
  19.6 12.7 %collective-permute-start.8 = (f32[64,1024]{1,0:T(8,128)}, f32[64,1024]{1,0:T(8,128)S(1)}, u32[]{:S(2)}, u32[]{:S(2)}) collective-permute-start(f32[64,1024]{1,0:T(8,128)} %get-tuple-element.17), channel_id=1, source_target_pairs={{0,32},{8,40},{1,33},{9,41},{2,34},{10,42},{3,35},{11,43},{4,36},{... | collective-permute-start | bytes 786440 | tf_op jit(solution)/shard_map/ppermute | solution.py:37
  20.9 11.4 %collective-permute-start.7 = (f32[64,1024]{1,0:T(8,128)}, f32[64,1024]{1,0:T(8,128)}, u32[]{:S(2)}, u32[]{:S(2)}) collective-permute-start(f32[64,1024]{1,0:T(8,128)} %get-tuple-element.18), channel_id=1, source_target_pairs={{0,16},{8,24},{1,17},{9,25},{2,18},{10,26},{3,19},{11,27},{4,20},{... | collective-permute-start | bytes 786440 | tf_op jit(solution)/shard_map/ppermute | solution.py:37
  22.3 10.0 %collective-permute-start.9 = (f32[64,1024]{1,0:T(8,128)}, f32[64,1024]{1,0:T(8,128)}, u32[]{:S(2)}, u32[]{:S(2)}) collective-permute-start(f32[64,1024]{1,0:T(8,128)} %get-tuple-element.19), channel_id=1, source_target_pairs={{0,48},{8,56},{1,49},{9,57},{2,50},{10,58},{3,51},{11,59},{4,52},{... | collective-permute-start | bytes 786440 | tf_op jit(solution)/shard_map/ppermute | solution.py:37
  23.9 19.7 %collective-permute-start.2 = (f32[64,1024]{1,0:T(8,128)S(1)}, f32[64,1024]{1,0:T(8,128)S(1)}, u32[]{:S(2)}, u32[]{:S(2)}) collective-permute-start(f32[64,1024]{1,0:T(8,128)S(1)} %get-tuple-element.22), channel_id=1, source_target_pairs={{0,32},{8,40},{16,48},{24,56},{32,0},{40,8},{48,16},{56,24},{64,96... | collective-permute-start | bytes 786440 | tf_op jit(solution)/shard_map/ppermute | solution.py:32
  29.4 15.5 %collective-permute-start.3 = (f32[64,1024]{1,0:T(8,128)S(1)}, f32[64,1024]{1,0:T(8,128)S(1)}, u32[]{:S(2)}, u32[]{:S(2)}) collective-permute-start(f32[64,1024]{1,0:T(8,128)S(1)} %get-tuple-element.23), channel_id=1, source_target_pairs={{0,48},{8,56},{16,0},{24,8},{32,16},{40,24},{48,32},{56,40},{64,11... | collective-permute-start | bytes 786440 | tf_op jit(solution)/shard_map/ppermute | solution.py:32
  32.3 13.1 %collective-permute-start.1 = (f32[64,1024]{1,0:T(8,128)S(1)}, f32[64,1024]{1,0:T(8,128)S(1)}, u32[]{:S(2)}, u32[]{:S(2)}) collective-permute-start(f32[64,1024]{1,0:T(8,128)S(1)} %get-tuple-element.24), channel_id=1, source_target_pairs={{0,16},{8,24},{16,32},{24,40},{32,48},{40,56},{48,0},{56,8},{64,80... | collective-permute-start | bytes 786440 | tf_op jit(solution)/shard_map/ppermute | solution.py:32
  33.5 13.0 %collective-permute-start.11 = (f32[16,1024]{1,0:T(8,128)S(1)}, f32[16,1024]{1,0:T(8,128)S(1)}, u32[]{:S(2)}, u32[]{:S(2)}) collective-permute-start(f32[16,1024]{1,0:T(8,128)S(1)} %get-tuple-element.27), channel_id=1, source_target_pairs={{0,128},{8,136},{16,144},{24,152},{32,160},{40,168},{48,176},{56,1... | collective-permute-start | bytes 196616 | tf_op jit(solution)/shard_map/ppermute | solution.py:37
  36.5 12.9 %collective-permute-start.12 = (f32[16,1024]{1,0:T(8,128)S(1)}, f32[16,1024]{1,0:T(8,128)S(1)}, u32[]{:S(2)}, u32[]{:S(2)}) collective-permute-start(f32[16,1024]{1,0:T(8,128)S(1)} %get-tuple-element.28), channel_id=1, source_target_pairs={{0,192},{8,200},{16,208},{24,216},{32,224},{40,232},{48,240},{56,2... | collective-permute-start | bytes 196616 | tf_op jit(solution)/shard_map/ppermute | solution.py:37
  43.6 5.8 %collective-permute-start.10 = (f32[16,1024]{1,0:T(8,128)S(1)}, f32[16,1024]{1,0:T(8,128)S(1)}, u32[]{:S(2)}, u32[]{:S(2)}) collective-permute-start(f32[16,1024]{1,0:T(8,128)S(1)} %get-tuple-element.29), channel_id=1, source_target_pairs={{0,64},{8,72},{16,80},{24,88},{32,96},{40,104},{48,112},{56,120},{... | collective-permute-start | bytes 196616 | tf_op jit(solution)/shard_map/ppermute | solution.py:37
  45.5 9.3 %collective-permute-start.5 = (f32[16,1024]{1,0:T(8,128)S(1)}, f32[16,1024]{1,0:T(8,128)S(1)}, u32[]{:S(2)}, u32[]{:S(2)}) collective-permute-start(f32[16,1024]{1,0:T(8,128)S(1)} %get-tuple-element.30), channel_id=1, source_target_pairs={{0,128},{8,136},{16,144},{24,152},{32,160},{40,168},{48,176},{56,1... | collective-permute-start | bytes 196616 | tf_op jit(solution)/shard_map/ppermute | solution.py:32
  46.5 8.4 %collective-permute-start.6 = (f32[16,1024]{1,0:T(8,128)S(1)}, f32[16,1024]{1,0:T(8,128)S(1)}, u32[]{:S(2)}, u32[]{:S(2)}) collective-permute-start(f32[16,1024]{1,0:T(8,128)S(1)} %get-tuple-element.31), channel_id=1, source_target_pairs={{0,192},{8,200},{16,208},{24,216},{32,224},{40,232},{48,240},{56,2... | collective-permute-start | bytes 196616 | tf_op jit(solution)/shard_map/ppermute | solution.py:32
  46.5 9.1 %collective-permute-start.4 = (f32[16,1024]{1,0:T(8,128)S(1)}, f32[16,1024]{1,0:T(8,128)S(1)}, u32[]{:S(2)}, u32[]{:S(2)}) collective-permute-start(f32[16,1024]{1,0:T(8,128)S(1)} %get-tuple-element.32), channel_id=1, source_target_pairs={{0,64},{8,72},{16,80},{24,88},{32,96},{40,104},{48,112},{56,120},{... | collective-permute-start | bytes 196616 | tf_op jit(solution)/shard_map/ppermute | solution.py:32
  56.4 12.6 %all-to-all-start.1 = ((f32[8,32,256]{2,1,0:T(8,128)}), f32[8,32,256]{2,1,0:T(8,128)S(1)}, u32[]{:S(2)}, u32[]{:S(2)}) async-start(f32[8,32,256]{2,1,0:T(8,128)} %tile.2), calls=%async_computation.1 | async-start | bytes 524288 | tf_op jit(solution)/shard_map/all_to_all | solution.py:249
  69.0 40.0 %all-to-all-start = ((f32[8,160,256]{2,1,0:T(8,128)}), f32[8,160,256]{2,1,0:T(8,128)S(1)}, u32[]{:S(2)}, u32[]{:S(2)}) async-start(f32[8,160,256]{2,1,0:T(8,128)} %bitcast.5), calls=%async_computation | async-start | bytes 2621440 | tf_op jit(solution)/shard_map/all_to_all | solution.py:229
  72.6 85.0 %all-gather.2.cloned.1.call-start = ((), (), s32[]{:S(2)}) async-start(), calls=%async_computation.2 | async-start | bytes 2949120 | tf_op jit(solution)/shard_map/all_gather | solution.py:232
  73.9 8.0 %collective-permute-start.15 = (f32[16,2816]{1,0:T(8,128)S(1)}, f32[16,2816]{1,0:T(8,128)S(1)}, u32[]{:S(2)}, u32[]{:S(2)}) collective-permute-start(f32[16,2816]{1,0:T(8,128)S(1)} %get-tuple-element.25), channel_id=1, source_target_pairs={{0,192},{8,200},{16,208},{24,216},{32,224},{40,232},{48,240},{56,2... | collective-permute-start | bytes 540680 | tf_op jit(solution)/shard_map/ppermute | solution.py:32
  76.4 22.9 %collective-permute-start.14 = (f32[16,2816]{1,0:T(8,128)S(1)}, f32[16,2816]{1,0:T(8,128)S(1)}, u32[]{:S(2)}, u32[]{:S(2)}) collective-permute-start(f32[16,2816]{1,0:T(8,128)S(1)} %get-tuple-element.25), channel_id=1, source_target_pairs={{0,128},{8,136},{16,144},{24,152},{32,160},{40,168},{48,176},{56,1... | collective-permute-start | bytes 540680 | tf_op jit(solution)/shard_map/ppermute | solution.py:32
  78.3 23.7 %collective-permute-start.13 = (f32[16,2816]{1,0:T(8,128)S(1)}, f32[16,2816]{1,0:T(8,128)S(1)}, u32[]{:S(2)}, u32[]{:S(2)}) collective-permute-start(f32[16,2816]{1,0:T(8,128)S(1)} %get-tuple-element.25), channel_id=1, source_target_pairs={{0,64},{8,72},{16,80},{24,88},{32,96},{40,104},{48,112},{56,120},{... | collective-permute-start | bytes 540680 | tf_op jit(solution)/shard_map/ppermute | solution.py:32
  102.1 38.0 %collective-permute-start.18 = (f32[64,2816]{1,0:T(8,128)S(1)}, f32[64,2816]{1,0:T(8,128)S(1)}, u32[]{:S(2)}, u32[]{:S(2)}) collective-permute-start(f32[64,2816]{1,0:T(8,128)S(1)} %pad_maximum_fusion), channel_id=1, source_target_pairs={{0,48},{8,56},{16,0},{24,8},{32,16},{40,24},{48,32},{56,40},{64,11... | collective-permute-start | bytes 2162696 | tf_op jit(solution)/shard_map/ppermute | solution.py:32
  106.1 33.0 %collective-permute-start.17 = (f32[64,2816]{1,0:T(8,128)S(1)}, f32[64,2816]{1,0:T(8,128)S(1)}, u32[]{:S(2)}, u32[]{:S(2)}) collective-permute-start(f32[64,2816]{1,0:T(8,128)S(1)} %pad_maximum_fusion), channel_id=1, source_target_pairs={{0,32},{8,40},{16,48},{24,56},{32,0},{40,8},{48,16},{56,24},{64,96... | collective-permute-start | bytes 2162696 | tf_op jit(solution)/shard_map/ppermute | solution.py:32
  106.2 30.8 %collective-permute-start.16 = (f32[64,2816]{1,0:T(8,128)S(1)}, f32[64,2816]{1,0:T(8,128)}, u32[]{:S(2)}, u32[]{:S(2)}) collective-permute-start(f32[64,2816]{1,0:T(8,128)S(1)} %pad_maximum_fusion), channel_id=1, source_target_pairs={{0,16},{8,24},{16,32},{24,40},{32,48},{40,56},{48,0},{56,8},{64,80... | collective-permute-start | bytes 2162696 | tf_op jit(solution)/shard_map/ppermute | solution.py:32
  109.0 48.5 %copy-start.1 = (f32[2,256,256]{2,1,0:T(8,128)S(1)}, f32[2,256,256]{2,1,0:T(8,128)}, u32[]{:S(2)}) copy-start(f32[2,256,256]{2,1,0:T(8,128)} %m_ref.1) | copy-start | bytes 1572868
  141.0 5.6 %collective-permute-start.19 = (f32[256,2816]{1,0:T(8,128)}, f32[256,2816]{1,0:T(8,128)}, u32[]{:S(2)}, u32[]{:S(2)}) collective-permute-start(f32[256,2816]{1,0:T(8,128)} %constant_dynamic-update-slice_fusion.5.g0_ref), channel_id=1, source_target_pairs={{0,8},{8,0},{16,24},{24,16},{32,40},{40,32},{48,56},{56,48},{64,72... | collective-permute-start | bytes 8650760 | tf_op jit(solution)/shard_map/ppermute | solution.py:32
  (5 other events, 86.4 us)
Sparse Core Ops, SparseCore 0:
  110.0 47.5 all-gather.1

commit v2 on v1

v2 whole, which is shorter than its diff:
```python
import functools

import jax
import jax.numpy as jnp
from jax import lax
from jax.experimental import pallas as pl
from jax.experimental.pallas import tpu as pltpu
from jax.sharding import PartitionSpec as P

NB = 256
ROWS_DEV = 1280
COLS_DEV = 1024
XS = 4
ZS = 4
QUARTER = NB // XS
SUB = QUARTER // ZS
BLOCK = 256
PART = ROWS_DEV // 8
HALF = 32


def shift(core, x, z):
    pairs = []
    for index in range(2 * XS * ZS):
        c, xi, zi = index % 2, index // 2 % XS, index // (2 * XS)
        target = ((zi + z) % ZS * XS + (xi + x) % XS) * 2 + (c + core) % 2
        pairs.append((index, target))
    return pairs


def send(value, core=0, x=0, z=0):
    return lax.ppermute(value, "prow", shift(core, x, z))


def send_from(value, keep, core=0, x=0, z=0):
    pairs = [pair for pair in shift(core, x, z) if keep(pair[0] // 2 % XS, pair[0] // (2 * XS))]
    return lax.ppermute(value, "prow", pairs)


def owned_rows(pivots, prow, number):
    local = pivots.reshape(2 * NB) - prow * ROWS_DEV
    owned = (local >= 0) & (local < ROWS_DEV)
    index = lax.broadcasted_iota(jnp.int32, (2 * NB, 2 * NB), 0)
    other = lax.broadcasted_iota(jnp.int32, (2 * NB, 2 * NB), 1)
    before = jnp.sum(jnp.where(owned[None, :] & (other < index), 1, 0), axis=1)
    slot = jnp.where(owned, before, 2 * NB)
    packed = local * (2 * NB) + number
    entries = jnp.sum(jnp.where(slot[None, :] == index, packed[None, :], 0), axis=1)
    return entries, jnp.sum(jnp.where(owned, 1, 0)).reshape(1)


def pick_kernel(place, entries, count, a_ref, mine, theirs, panel, top, sem, panel_sem, top_sem):
    x, z, core = place[1], place[2], place[3]
    panel_copy = pltpu.make_async_copy(a_ref.at[:, :NB], panel, panel_sem)
    top_copy = pltpu.make_async_copy(a_ref.at[:NB, :], top, top_sem)
    panel_copy.start()
    top_copy.start()
    mine[...] = jnp.zeros_like(mine)
    theirs[...] = jnp.zeros_like(theirs)

    def start(n, carry):
        local, number = entries[n] // (2 * NB), entries[n] % (2 * NB)
        i = number % NB
        quarter, sub, low = i // QUARTER, i // SUB % ZS, i % SUB
        dest = (quarter - x + XS) % XS * QUARTER + (sub - z + ZS) % ZS * SUB + low
        own = core == number // NB
        row = a_ref.at[pl.ds(local, 1), :]

        @pl.when(own)
        def _():
            pltpu.make_async_copy(row, mine.at[pl.ds(dest, 1), :], sem).start()

        @pl.when(jnp.logical_not(own))
        def _():
            pltpu.make_async_copy(row, theirs.at[pl.ds(dest, 1), :], sem).start()

        return carry

    def wait(n, carry):
        pltpu.make_async_copy(a_ref.at[pl.ds(0, 1), :], mine.at[pl.ds(0, 1), :], sem).wait()
        return carry

    lax.fori_loop(0, count[0], start, 0)
    lax.fori_loop(0, count[0], wait, 0)
    panel_copy.wait()
    top_copy.wait()


def pick(place, entries, count, matrix):
    smem = pl.BlockSpec(memory_space=pltpu.SMEM)
    vmem = pl.BlockSpec(memory_space=pltpu.VMEM)
    half = jax.ShapeDtypeStruct((NB, COLS_DEV), jnp.float32)
    return pl.pallas_call(
        pick_kernel,
        out_shape=[half, half, jax.ShapeDtypeStruct((ROWS_DEV, NB), jnp.float32), half],
        in_specs=[smem, smem, smem, pl.BlockSpec(memory_space=pltpu.HBM)],
        out_specs=[vmem] * 4,
        scratch_shapes=[pltpu.SemaphoreType.DMA] * 3,
        compiler_params=pltpu.CompilerParams(vmem_limit_bytes=8 * 1024 * 1024),
        name="pick_rows",
    )(place, entries, count, matrix)


def split(value):
    high = value.astype(jnp.bfloat16)
    low = (value - high.astype(jnp.float32)).astype(jnp.bfloat16)
    return high, low


def mul(a, b):
    dot = functools.partial(jnp.dot, preferred_element_type=jnp.float32)
    return dot(a[0], b[0]) + (dot(a[0], b[1]) + dot(a[1], b[0]))


def three(value):
    high, rest = value.astype(jnp.bfloat16), None
    rest = value - high.astype(jnp.float32)
    middle = rest.astype(jnp.bfloat16)
    return high, middle, (rest - middle.astype(jnp.float32)).astype(jnp.bfloat16)


def spread_kernel(place, own_ref, other_ref, pick_own, pick_other, *refs):
    outs = refs[-XS:]

    @pl.when((place[1] == 0) & (place[2] == 0))
    def _():
        rows = ZS * HALF
        for n in range(COLS_DEV // NB):
            cols = slice(n * NB, (n + 1) * NB)
            own, other = three(own_ref[:, cols]), three(other_ref[:, cols])
            for j in range(XS):
                block = slice(j * rows, (j + 1) * rows)
                dot = functools.partial(jnp.dot, preferred_element_type=jnp.float32)
                total = [
                    dot(pick_own[block, :], a) + dot(pick_other[block, :], b)
                    for a, b in zip(own, other)
                ]
                outs[j][:, cols] = total[0] + (total[1] + total[2])


def spread(place, own, other, picks, tokens):
    smem, vmem = pl.BlockSpec(memory_space=pltpu.SMEM), pl.BlockSpec(memory_space=pltpu.VMEM)
    anywhere = pl.BlockSpec(memory_space=pl.ANY)
    shape = jax.ShapeDtypeStruct((ZS * HALF, COLS_DEV), jnp.float32)
    return pl.pallas_call(
        spread_kernel,
        out_shape=[shape] * XS,
        in_specs=[smem, vmem, vmem, vmem, vmem] + [anywhere] * len(tokens),
        out_specs=[vmem] * XS,
        compiler_params=pltpu.CompilerParams(vmem_limit_bytes=16 * 1024 * 1024),
        name="spread_rows",
    )(place, own, other, *picks, *tokens)


def choose_kernel(axis, tokens, place, *refs):
    pieces, outs = refs[:4], refs[4 + tokens:]
    rows = outs[0].shape[0]
    for n, piece in enumerate(pieces):

        @pl.when(place[axis] == n)
        def _():
            for i, out in enumerate(outs):
                out[...] = piece[i * rows:(i + 1) * rows, :]


def choose(place, axis, pieces, count, tokens):
    smem, vmem = pl.BlockSpec(memory_space=pltpu.SMEM), pl.BlockSpec(memory_space=pltpu.VMEM)
    anywhere = pl.BlockSpec(memory_space=pl.ANY)
    rows, cols = pieces[0].shape
    return pl.pallas_call(
        functools.partial(choose_kernel, axis, len(tokens)),
        out_shape=[jax.ShapeDtypeStruct((rows // count, cols), jnp.float32)] * count,
        in_specs=[smem] + [vmem] * 4 + [anywhere] * len(tokens),
        out_specs=[vmem] * count,
        compiler_params=pltpu.CompilerParams(vmem_limit_bytes=8 * 1024 * 1024),
        name="choose_piece",
    )(place, *pieces, *tokens)


def update_kernel(
    packed, place, entries, count, a_ref, p_ref, m_ref, w_ref, *refs
):
    pieces, displaced = refs[:2 * XS], refs[2 * XS:-10]
    out_ref, xs, uh, ul, top, ph, wh, wl, ch, cl = refs[-10:]
    prow, x, z, core, pcol = place[0], place[1], place[2], place[3], place[4]
    block = pl.program_id(0)

    @pl.when(block == 0)
    def _():
        for piece in range(2 * XS):
            step = core if piece < XS else 1 - core
            for k in range(ZS):
                dest = step * NB + (x - piece + 2 * XS) % XS * QUARTER + (z - k + ZS) % ZS * SUB
                dest = pl.multiple_of(dest, SUB)
                xs[pl.ds(dest, SUB), :] = pieces[piece][k * SUB:(k + 1) * SUB, :]
        w0, w1 = split(w_ref[0]), split(w_ref[1])
        wh[0], wl[0] = w0
        wh[1], wl[1] = w1
        m0, m1 = split(m_ref[0]), split(m_ref[1])
        l0r1 = mul(split(xs[NB:, COLS_DEV:]), w0)
        u0c1 = mul(m0, split(xs[:NB, COLS_DEV:]))
        ch[...], cl[...] = split(u0c1)
        l0r1s = split(l0r1)
        u0 = mul(m0, split(xs[:NB, :COLS_DEV]))
        u0s = split(u0)
        uh[:NB, :], ul[:NB, :] = u0s
        y1 = xs[NB:, :COLS_DEV] - mul(l0r1s, u0s)
        u1 = mul(m1, split(y1))
        uh[NB:, :], ul[NB:, :] = split(u1)

        @pl.when(prow == 0)
        def _():
            top[...] = u0

            @pl.when(pcol == 0)
            def _():
                top[:, :NB] = xs[:NB, :NB]

        @pl.when(prow == 1)
        def _():
            top[...] = u1

            @pl.when(pcol == 0)
            def _():
                top[:, :NB] = l0r1

            @pl.when(pcol == 1)
            def _():
                top[:, :NB] = y1[:, :NB]

    @pl.when((block == 0) & (prow < 2))
    def _():
        out_ref[...] = top[...]

    @pl.when((block > 0) | (prow >= 2))
    def _():
        out_ref[...] = a_ref[...]
        ph[...] = p_ref[...]
        base = block * BLOCK

        def patch(n, carry):
            local, number = entries[n] // (2 * NB) - base, entries[n] % (2 * NB)

            @pl.when((local >= 0) & (local < BLOCK))
            def _():
                if packed:
                    src = number % HALF
                    piece = jnp.where(core == number // HALF, 0, 1)
                else:
                    i = number % NB
                    src = (z - i // SUB % ZS + ZS) % ZS * SUB + i % SUB
                    piece = jnp.where(core == number // NB, 0, XS) + (x - i // QUARTER + XS) % XS
                for j in range(len(displaced)):

                    @pl.when(piece == j)
                    def _():
                        row = displaced[j][pl.ds(src, 1), :]
                        out_ref[pl.ds(local, 1), :] = row[:, :COLS_DEV]
                        ph[pl.ds(local, 1), :] = row[:, COLS_DEV:]

            return carry

        lax.fori_loop(0, count[0], patch, 0)
        w0, w1 = (wh[0], wl[0]), (wh[1], wl[1])
        l0 = mul(split(ph[:, :NB]), w0)
        l0s = split(l0)
        l1 = mul(split(ph[:, NB:] - mul(l0s, (ch[...], cl[...]))), w1)
        l1s = split(l1)
        ls = tuple(jnp.concatenate([a, b], axis=1) for a, b in zip(l0s, l1s))
        for n in range(COLS_DEV // NB):
            cols = slice(n * NB, (n + 1) * NB)
            out_ref[:, cols] = out_ref[:, cols] - mul(ls, (uh[:, cols], ul[:, cols]))

        @pl.when(pcol == 0)
        def _():
            out_ref[:, :NB] = l0

        @pl.when(pcol == 1)
        def _():
            out_ref[:, :NB] = l1


def update(packed, place, entries, count, matrix, panels, lower, upper, pieces, displaced):
    smem = pl.BlockSpec(memory_space=pltpu.SMEM)
    vmem = pl.BlockSpec(memory_space=pltpu.VMEM)
    f32, bf16 = jnp.float32, jnp.bfloat16
    wide = pl.BlockSpec((BLOCK, COLS_DEV), lambda i: (i, 0))
    return pl.pallas_call(
        functools.partial(update_kernel, packed),
        grid=(ROWS_DEV // BLOCK,),
        out_shape=jax.ShapeDtypeStruct((ROWS_DEV, COLS_DEV), f32),
        in_specs=[smem, smem, smem, wide, pl.BlockSpec((BLOCK, 2 * NB), lambda i: (i, 0))]
        + [vmem] * (2 + len(pieces) + len(displaced)),
        out_specs=wide,
        scratch_shapes=[
            pltpu.VMEM((2 * NB, COLS_DEV + NB), f32),
            pltpu.VMEM((2 * NB, COLS_DEV), bf16),
            pltpu.VMEM((2 * NB, COLS_DEV), bf16),
            pltpu.VMEM((NB, COLS_DEV), f32),
            pltpu.VMEM((BLOCK, 2 * NB), f32),
            pltpu.VMEM((2, NB, NB), bf16),
            pltpu.VMEM((2, NB, NB), bf16),
            pltpu.VMEM((NB, NB), bf16),
            pltpu.VMEM((NB, NB), bf16),
        ],
        compiler_params=pltpu.CompilerParams(vmem_limit_bytes=40 * 1024 * 1024),
        name="panel_update",
    )(place, entries, count, matrix, panels, lower, upper, *pieces, *displaced)


def add_kernel(n, tokens, *refs):
    parts, outs = refs[:n], refs[n + tokens:]
    rows = outs[0].shape[0]
    for i, out in enumerate(outs):
        block = slice(i * rows, (i + 1) * rows)
        value = parts[0][block, :]
        for part in parts[1:]:
            value = value + part[block, :]
        out[...] = value


def add(parts, count, tokens=()):
    vmem, anywhere = pl.BlockSpec(memory_space=pltpu.VMEM), pl.BlockSpec(memory_space=pl.ANY)
    rows, cols = parts[0].shape
    return pl.pallas_call(
        functools.partial(add_kernel, len(parts), len(tokens)),
        out_shape=[jax.ShapeDtypeStruct((rows // count, cols), jnp.float32)] * count,
        in_specs=[vmem] * len(parts) + [anywhere] * len(tokens),
        out_specs=[vmem] * count,
        compiler_params=pltpu.CompilerParams(vmem_limit_bytes=8 * 1024 * 1024),
        name="add_parts",
    )(*parts, *tokens)


def sync(*values):
    anywhere = pl.BlockSpec(memory_space=pl.ANY)
    return pl.pallas_call(
        lambda *refs: None,
        out_shape=[jax.ShapeDtypeStruct(value.shape, value.dtype) for value in values],
        in_specs=[anywhere] * len(values),
        out_specs=[anywhere] * len(values),
        input_output_aliases={i: i for i in range(len(values))},
        compiler_params=pltpu.CompilerParams(vmem_limit_bytes=1024 * 1024),
        name="sync",
    )(*values)


def pack_kernel(groups, count, *refs):
    parts, out = refs[:groups * count], refs[-1]
    col = 0
    for i in range(groups):
        rows, width = parts[i * count].shape
        for k in range(count):
            out[k * rows:(k + 1) * rows, col:col + width] = parts[i * count + k][...]
        col += width


def pack(groups, tokens=()):
    vmem, anywhere = pl.BlockSpec(memory_space=pltpu.VMEM), pl.BlockSpec(memory_space=pl.ANY)
    cols = sum(group[0].shape[1] for group in groups)
    parts = [part for group in groups for part in group]
    return pl.pallas_call(
        functools.partial(pack_kernel, len(groups), len(groups[0])),
        out_shape=jax.ShapeDtypeStruct((groups[0][0].shape[0] * len(groups[0]), cols), jnp.float32),
        in_specs=[vmem] * len(parts) + [anywhere] * len(tokens),
        out_specs=vmem,
        compiler_params=pltpu.CompilerParams(vmem_limit_bytes=8 * 1024 * 1024),
        name="pack_blocks",
    )(*parts, *tokens)


def gather_z(held):
    return [held] + [send(held, z=k) for k in range(1, ZS)]


def gather_x(held):
    pieces = [held] + [send(held, x=j) for j in range(1, XS)]
    return pieces + [send(piece, core=1) for piece in pieces]


def to_columns(value):
    rows = value.shape[0]
    value = lax.all_to_all(jnp.tile(value, (8, 1)), "pcol", 0, 0, tiled=True)
    return value[:rows], value[rows:2 * rows]


def panel_parts(panel):
    parts = lax.all_to_all(panel, "pcol", 0, 0, tiled=True)
    return jnp.concatenate([parts[:PART], parts[PART:2 * PART]], axis=1)


def panel_rows(parts):
    return lax.all_to_all(jnp.tile(parts, (8, 1)), "pcol", 0, 0, tiled=True)


def from_root(pieces, axis):
    keep = (lambda xi, zi: xi == 0 and zi == 0) if axis == "x" else (lambda xi, zi: zi == 0)
    return [pieces[0]] + [send_from(pieces[n], keep, **{axis: n}) for n in range(1, 4)]


def on_device(matrix, pivots, lower_inverse, upper_inverse):
    prow = lax.axis_index("prow")
    core, x, z = prow % 2, prow // 2 % XS, prow // (2 * XS)
    place = jnp.stack([prow, x, z, core, lax.axis_index("pcol")]).astype(jnp.int32)
    operands = (place, matrix, pivots, lower_inverse, upper_inverse)
    result, most = exchange(True, *operands)
    return lax.while_loop(
        lambda state: state[0],
        lambda state: (False, exchange(False, *operands)[0]),
        (most >= 2 * HALF, result),
    )[1]


def chip_places(pivots):
    number = lax.broadcasted_iota(jnp.int32, (2 * NB,), 0)
    chip = pivots.reshape(2 * NB) // (2 * ROWS_DEV)
    before = number[None, :] < number[:, None]
    return chip, jnp.sum(jnp.where(before & (chip[None, :] == chip[:, None]), 1, 0), axis=1)


def exchange(packed, place, matrix, pivots, lower_inverse, upper_inverse):
    prow, core = place[0], place[3]

    number = lax.broadcasted_iota(jnp.int32, (2 * NB,), 0)
    entries, count = owned_rows(pivots, prow, number)
    mine, theirs, panel, top = pick(place, entries, count, matrix)
    parts = panel_parts(panel)
    theirs, pivots = sync(theirs, pivots)
    chip, rank = chip_places(pivots)
    summed = add([mine, send(theirs, core=1)], XS)
    received = [send(summed[j], x=j) for j in range(1, XS)]

    if packed:
        other = send_from(top, lambda xi, zi: xi == 0 and zi == 0, core=1)
        where = (chip % XS * ZS + chip // XS) * HALF + rank % HALF
        where = jnp.where(rank // HALF == core, where, -1).reshape(2, 1, NB)
        index = lax.broadcasted_iota(jnp.int32, (XS * ZS * HALF, NB), 0)
        steps = [jnp.where(core == 0, where[k], where[1 - k]) for k in range(2)]
        picks = [(index == step).astype(jnp.bfloat16) for step in steps]
        quarters = spread(place, top, other, picks, summed[:1])
    else:
        quarters = add([top], XS)
    total = add([summed[0]] + received, ZS)
    *total, parts = sync(*total, parts)

    panels = panel_rows(parts)
    received = [send(total[k], z=k) for k in range(1, ZS)]
    total, *quarters = sync(add([total[0]] + received, 1)[0], *quarters)

    blocks = gather_z(total)
    panels, columns = sync(panels, total[:, :NB])
    from_0, from_1 = to_columns(columns)
    crossed = jnp.where(core == 0, from_1, from_0)
    subs = choose(place, 1, from_root(quarters, "x"), ZS, [])
    values = sync(*blocks, crossed, *subs)
    blocks, crossed, subs = values[:ZS], values[ZS], values[ZS + 1:]

    (displaced,) = choose(place, 2, from_root(subs, "z"), 1, [])
    total, displaced = sync(pack([blocks, gather_z(crossed)]), displaced)

    total = gather_x(total)
    columns = [[part] for part in to_columns(displaced[:, :NB])]
    displaced = pack([[displaced]] + columns)
    if packed:
        entries, _ = owned_rows(pivots, prow, rank)
        displaced = [displaced, send(displaced, core=1)]
    else:
        displaced = gather_x(pack([gather_z(displaced)]))
    result = update(
        packed, place, entries, count, matrix, panels, lower_inverse, upper_inverse,
        total, displaced,
    )
    return result, jnp.max(rank)


def solution(mesh):
    in_specs = (P("prow", "pcol"), P(), P(), P())
    out_specs = P("prow", "pcol")
    return jax.shard_map(
        on_device, mesh=mesh, in_specs=in_specs, out_specs=out_specs, check_vma=False
    )
```

time: 185 us -> 168 us (0.908); the launches traced: 184 us -> 165 us
  waiting for transfers between devices: 80.9 us -> 62 us
  starting transfers between devices: 40.5 us -> 58 us
  between operations: 13.6 us -> 1.06 us
  local copies, waits for them, and re-layouts: 18.1 us -> 10.4 us
  other arithmetic: 2.85 us -> 5.71 us
    all_to_all x2 -> x4, starting transfers between devices: 8.98 us -> 20.5 us  [the longest x2 8.86 us: to_columns(): value = lax.all_to_all(jnp.tile(value, (8, 1)), 'pcol', 0, 0, tiled=True)]
    all_gather x1 -> x0, waiting for transfers between devices: 11 us -> none  [on_device(): panels = lax.all_gather(panels, 'pcol', tiled=True)]
    ppermute x14 -> x21, waiting for transfers between devices: 62.2 us -> 54.4 us  [send(): return lax.ppermute(value, 'prow', shift(core, x, z))]
    ppermute x14 -> x21, starting transfers between devices: 21.9 us -> 27.8 us  [send(): return lax.ppermute(value, 'prow', shift(core, x, z))]
    unnamed x23 -> x24, local copies, waits for them, and re-layouts: 11.8 us -> 5.97 us
    all_to_all x2 -> x4, waiting for transfers between devices: 4.77 us -> 0.01 us  [the longest x2 0.01 us: to_columns(): value = lax.all_to_all(jnp.tile(value, (8, 1)), 'pcol', 0, 0, tiled=True)]
    ppermute x6 -> x7, waiting for transfers between devices: 2.95 us -> 7.58 us  [send_from(): return lax.ppermute(value, 'prow', pairs)]
    slice x8 -> x4, local copies, waits for them, and re-layouts: 4.59 us -> 1.03 us  [the longest x1 1.02 us: panel_parts(): return jnp.concatenate([parts[:PART], parts[PART:2 * PART]], axis=1)]
  transfers between devices with their start and end apart: 23 -> 32, of which waited for: 11 -> 12; matrix products, arithmetic and copies ran while one was open for 10% -> 3% of each run, Pallas kernels for 0% -> 3%
where the time goes in v2:
time: 168 us; the launch traced here: 165 us
  waiting for transfers between devices  62 us (37%)
  starting transfers between devices  58 us (35%)
  Pallas kernels  27.5 us (16%)
  local copies, waits for them, and re-layouts  10.4 us (6%)
  other arithmetic  5.71 us (3%)
    ppermute x21, waiting for transfers between devices, send(): return lax.ppermute(value, 'prow', shift(core, x, z))  54.4 us
    ppermute x21, starting transfers between devices, send(): return lax.ppermute(value, 'prow', shift(core, x, z))  27.8 us
    pallas_call x1, Pallas kernels, update(): pl.pallas_call(functools.partial(update_kernel, packed), grid=(ROWS_DEV /...  17.5 us
    ppermute x7, starting transfers between devices, send_from(): return lax.ppermute(value, 'prow', pairs)  9.72 us
    all_to_all x2, starting transfers between devices, to_columns(): value = lax.all_to_all(jnp.tile(value, (8, 1)), 'pcol', 0, 0, tiled=True)  8.86 us
    ppermute x7, waiting for transfers between devices, send_from(): return lax.ppermute(value, 'prow', pairs)  7.58 us
    unnamed x24, local copies, waits for them, and re-layouts  5.97 us
    all_to_all x1, starting transfers between devices, panel_parts(): parts = lax.all_to_all(panel, 'pcol', 0, 0, tiled=True)  5.96 us
  transfers between devices with their start and end apart: 32, of which 12 were waited for; matrix products, arithmetic and copies ran while one was open for 3% of the time, Pallas kernels for 3%

profile of v2, /device:TPU:4, one launch (start us, length us, event | category | flops | bytes accessed | tf_op | source)
XLA Modules:
  0.0 164.7 jit_solution(4159930571374236874)
XLA Ops:
  1.8 4.1 %pick_rows.3 = (f32[256,1024]{1,0:T(8,128)S(1)}, f32[256,1024]{1,0:T(8,128)S(1)}, f32[1280,256]{1,0:T(8,128)}, f32[256,1024]{1,0:T(8,128)S(1)}) custom-call(s32[5]{0:T(128)S(1)} %stack.23.place, s32[512]{0:T(512)S(1)} %select_reduce_fusion.6.entries, s32[1]{0:T(128)} %bitcast.13.count, f32[1280,1024]{1,0:T(8,128)} %a_ref.3), custom_call_target="tpu_custom_call" | custom-call | tf_op jit(solution)/shard_map/pick_rows/pallas_call | solution.py:93
  6.9 6.0 %all-to-all-start.4 = ((f32[8,160,256]{2,1,0:T(8,128)}), f32[8,160,256]{2,1,0:T(8,128)}, u32[]{:S(2)}, u32[]{:S(2)}) async-start(f32[8,160,256]{2,1,0:T(8,128)} %bitcast.14), calls=%async_computation.4 | async-start | bytes 2621440 | tf_op jit(solution)/shard_map/all_to_all | solution.py:388
  13.0 2.6 %collective-permute-done.36.refs_1_ = f32[256,1024]{1,0:T(8,128)S(1)} collective-permute-done((f32[256,1024]{1,0:T(8,128)S(1)}, f32[256,1024]{1,0:T(8,128)S(1)}, u32[]{:S(2)}, u32[]{:S(2)}) %collective-permute-start.36) | collective-permute-done | bytes 1048608 | tf_op jit(solution)/shard_map/ppermute | solution.py:32
  19.0 10.7 %collective-permute-done.37.refs_1_ = f32[64,1024]{1,0:T(8,128)S(1)} collective-permute-done((f32[64,1024]{1,0:T(8,128)S(1)}, f32[64,1024]{1,0:T(8,128)S(1)}, u32[]{:S(2)}, u32[]{:S(2)}) %collective-permute-start.37) | collective-permute-done | bytes 262176 | tf_op jit(solution)/shard_map/ppermute | solution.py:32
  29.8 1.8 %collective-permute-done.39.refs_3_ = f32[64,1024]{1,0:T(8,128)S(1)} collective-permute-done((f32[64,1024]{1,0:T(8,128)S(1)}, f32[64,1024]{1,0:T(8,128)S(1)}, u32[]{:S(2)}, u32[]{:S(2)}) %collective-permute-start.39) | collective-permute-done | bytes 262176 | tf_op jit(solution)/shard_map/ppermute | solution.py:32
  35.2 5.7 %all-to-all-start.5 = ((f32[8,160,512]{2,1,0:T(8,128)}), f32[8,160,512]{2,1,0:T(8,128)S(1)}, u32[]{:S(2)}, u32[]{:S(2)}) async-start(f32[8,160,512]{2,1,0:T(8,128)} %tile.12), calls=%async_computation.5 | async-start | bytes 5242880 | tf_op jit(solution)/shard_map/all_to_all | solution.py:393
  44.2 3.3 %collective-permute-start.40 = (f32[16,1024]{1,0:T(8,128)S(1)}, f32[16,1024]{1,0:T(8,128)S(1)}, u32[]{:S(2)}, u32[]{:S(2)}) collective-permute-start(f32[16,1024]{1,0:T(8,128)S(1)} %get-tuple-element.154), channel_id=1, source_target_pairs={{0,64},{8,72},{16,80},{24,88},{32,96},{40,104},{48,112},{56,120},{... | collective-permute-start | bytes 196616 | tf_op jit(solution)/shard_map/ppermute | solution.py:32
  47.5 4.6 %collective-permute-start.41 = (f32[16,1024]{1,0:T(8,128)}, f32[16,1024]{1,0:T(8,128)S(1)}, u32[]{:S(2)}, u32[]{:S(2)}) collective-permute-start(f32[16,1024]{1,0:T(8,128)} %get-tuple-element.155), channel_id=1, source_target_pairs={{0,128},{8,136},{16,144},{24,152},{32,160},{40,168},{48,176},{56,1... | collective-permute-start | bytes 196616 | tf_op jit(solution)/shard_map/ppermute | solution.py:32
  52.1 2.8 %collective-permute-start.42 = (f32[16,1024]{1,0:T(8,128)}, f32[16,1024]{1,0:T(8,128)S(1)}, u32[]{:S(2)}, u32[]{:S(2)}) collective-permute-start(f32[16,1024]{1,0:T(8,128)} %get-tuple-element.156), channel_id=1, source_target_pairs={{0,192},{8,200},{16,208},{24,216},{32,224},{40,232},{48,240},{56,2... | collective-permute-start | bytes 196616 | tf_op jit(solution)/shard_map/ppermute | solution.py:32
  56.2 2.4 %spread_rows.1 = (f32[128,1024]{1,0:T(8,128)S(1)}, f32[128,1024]{1,0:T(8,128)}, f32[128,1024]{1,0:T(8,128)}, f32[128,1024]{1,0:T(8,128)}) custom-call(s32[5]{0:T(128)S(1)} %stack.23.place, f32[256,1024]{1,0:T(8,128)S(1)} %copy-done.11, f32[256,1024]{1,0:T(8,128)} %collective-permute-done.43.other_ref, bf16[512,256]{1,0:T(8,128)(2,1)S(1)} %fusion.5.pick_own, ...), custom_call_target="tpu_custom_call" | custom-call | tf_op jit(solution)/shard_map/spread_rows/pallas_call | solution.py:145
  58.5 20.0 %collective-permute-done.40.refs_1_ = f32[16,1024]{1,0:T(8,128)S(1)} collective-permute-done((f32[16,1024]{1,0:T(8,128)S(1)}, f32[16,1024]{1,0:T(8,128)S(1)}, u32[]{:S(2)}, u32[]{:S(2)}) %collective-permute-start.40) | collective-permute-done | bytes 65568 | tf_op jit(solution)/shard_map/ppermute | solution.py:32
  78.5 2.4 %collective-permute-done.41.refs_2_ = f32[16,1024]{1,0:T(8,128)S(1)} collective-permute-done((f32[16,1024]{1,0:T(8,128)}, f32[16,1024]{1,0:T(8,128)S(1)}, u32[]{:S(2)}, u32[]{:S(2)}) %collective-permute-start.41) | collective-permute-done | bytes 65568 | tf_op jit(solution)/shard_map/ppermute | solution.py:32
  85.9 4.6 %all-to-all-start.6 = ((f32[8,16,256]{2,1,0:T(8,128)}), f32[8,16,256]{2,1,0:T(8,128)}, u32[]{:S(2)}, u32[]{:S(2)}) async-start(f32[8,16,256]{2,1,0:T(8,128)} %tile.13), calls=%async_computation.6 | async-start | bytes 262144 | tf_op jit(solution)/shard_map/all_to_all | solution.py:383
  93.4 3.6 %collective-permute-start.46 = (f32[16,1024]{1,0:T(8,128)S(1)}, f32[16,1024]{1,0:T(8,128)S(1)}, u32[]{:S(2)}, u32[]{:S(2)}) collective-permute-start(f32[16,1024]{1,0:T(8,128)S(1)} %get-tuple-element.162.refs_0_), channel_id=1, source_target_pairs={{0,192},{8,200},{16,208},{24,216},{32,224},{40,232},{48,240},{56,2... | collective-permute-start | bytes 196616 | tf_op jit(solution)/shard_map/ppermute | solution.py:32
  97.1 7.6 %collective-permute-done.48.refs_2_ = f32[128,1024]{1,0:T(8,128)} collective-permute-done((f32[128,1024]{1,0:T(8,128)}, f32[128,1024]{1,0:T(8,128)}, u32[]{:S(2)}, u32[]{:S(2)}) %collective-permute-start.48) | collective-permute-done | bytes 524320 | tf_op jit(solution)/shard_map/ppermute | solution.py:37
  104.6 2.1 %choose_piece.6 = (f32[32,1024]{1,0:T(8,128)S(1)}, f32[32,1024]{1,0:T(8,128)S(1)}, f32[32,1024]{1,0:T(8,128)}, f32[32,1024]{1,0:T(8,128)S(1)}) custom-call(s32[5]{0:T(128)S(1)} %stack.23.place, f32[128,1024]{1,0:T(8,128)S(1)} %get-tuple-element.165.refs_0_, f32[128,1024]{1,0:T(8,128)} %collective-permute-done.47.refs_1_, ...), custom_call_target="tpu_custom_call" | custom-call | tf_op jit(solution)/shard_map/choose_piece/pallas_call | solution.py:170
  115.6 5.7 %collective-permute-done.50.refs_5_ = f32[16,256]{1,0:T(8,128)S(1)} collective-permute-done((f32[16,256]{1,0:T(8,128)S(1)}, f32[16,256]{1,0:T(8,128)S(1)}, u32[]{:S(2)}, u32[]{:S(2)}) %collective-permute-start.50) | collective-permute-done | bytes 16416 | tf_op jit(solution)/shard_map/ppermute | solution.py:32
  121.4 1.9 %collective-permute-done.51.refs_6_ = f32[16,256]{1,0:T(8,128)S(1)} collective-permute-done((f32[16,256]{1,0:T(8,128)S(1)}, f32[16,256]{1,0:T(8,128)S(1)}, u32[]{:S(2)}, u32[]{:S(2)}) %collective-permute-start.51) | collective-permute-done | bytes 16416 | tf_op jit(solution)/shard_map/ppermute | solution.py:32
  123.3 2.7 %collective-permute-done.52.refs_7_ = f32[16,256]{1,0:T(8,128)S(1)} collective-permute-done((f32[16,256]{1,0:T(8,128)S(1)}, f32[16,256]{1,0:T(8,128)S(1)}, u32[]{:S(2)}, u32[]{:S(2)}) %collective-permute-start.52) | collective-permute-done | bytes 16416 | tf_op jit(solution)/shard_map/ppermute | solution.py:32
  127.4 4.3 %all-to-all-start.7 = ((f32[8,32,256]{2,1,0:T(8,128)}), f32[8,32,256]{2,1,0:T(8,128)S(1)}, u32[]{:S(2)}, u32[]{:S(2)}) async-start(f32[8,32,256]{2,1,0:T(8,128)} %tile.14), calls=%async_computation.7 | async-start | bytes 524288 | tf_op jit(solution)/shard_map/all_to_all | solution.py:383
  131.7 3.5 %collective-permute-start.57 = (f32[64,1280]{1,0:T(8,128)S(1)}, f32[64,1280]{1,0:T(8,128)}, u32[]{:S(2)}, u32[]{:S(2)}) collective-permute-start(f32[64,1280]{1,0:T(8,128)S(1)} %get-tuple-element.182.refs_0_), channel_id=1, source_target_pairs={{0,32},{8,40},{16,48},{24,56},{32,0},{40,8},{48,16},{56,24},{64,96... | collective-permute-start | bytes 983048 | tf_op jit(solution)/shard_map/ppermute | solution.py:32
  135.2 2.5 %collective-permute-start.58 = (f32[64,1280]{1,0:T(8,128)S(1)}, f32[64,1280]{1,0:T(8,128)}, u32[]{:S(2)}, u32[]{:S(2)}) collective-permute-start(f32[64,1280]{1,0:T(8,128)S(1)} %get-tuple-element.182.refs_0_), channel_id=1, source_target_pairs={{0,48},{8,56},{16,0},{24,8},{32,16},{40,24},{48,32},{56,40},{64,11... | collective-permute-start | bytes 983048 | tf_op jit(solution)/shard_map/ppermute | solution.py:32
  139.0 4.8 %collective-permute-done.57.refs_2_ = f32[64,1280]{1,0:T(8,128)} collective-permute-done((f32[64,1280]{1,0:T(8,128)S(1)}, f32[64,1280]{1,0:T(8,128)}, u32[]{:S(2)}, u32[]{:S(2)}) %collective-permute-start.57) | collective-permute-done | bytes 327712 | tf_op jit(solution)/shard_map/ppermute | solution.py:32
  147.2 17.5 %panel_update.3 = f32[1280,1024]{1,0:T(8,128)} custom-call(s32[5]{0:T(128)S(1)} %stack.23.place, s32[512]{0:T(512)S(1)} %select_reduce_fusion.3.entries, s32[1]{0:T(128)} %bitcast.13.count, f32[1280,1024]{1,0:T(8,128)} %a_ref.3, f32[1280,512]{1,0:T(8,128)S(1)} %get-tuple-element.163.p_ref, f32[2,256,256]{2,1,0:T(8,128)} %m_ref.1, f32[2,256,256]{2,1,0:T(8,128)} %w_ref.1, ...), custom_call_target="tpu_custom_call" | custom-call | tf_op jit(solution)/shard_map/panel_update/pallas_call | solution.py:288
  (109 shorter events, 36.3 us)
Async XLA Ops:
  6.9 25.4 %all-to-all-start.4 = ((f32[8,160,256]{2,1,0:T(8,128)}), f32[8,160,256]{2,1,0:T(8,128)}, u32[]{:S(2)}, u32[]{:S(2)}) async-start(f32[8,160,256]{2,1,0:T(8,128)} %bitcast.14), calls=%async_computation.4 | async-start | bytes 2621440 | tf_op jit(solution)/shard_map/all_to_all | solution.py:388
  15.7 14.0 %collective-permute-start.37 = (f32[64,1024]{1,0:T(8,128)S(1)}, f32[64,1024]{1,0:T(8,128)S(1)}, u32[]{:S(2)}, u32[]{:S(2)}) collective-permute-start(f32[64,1024]{1,0:T(8,128)S(1)} %get-tuple-element.144), channel_id=1, source_target_pairs={{0,16},{8,24},{16,32},{24,40},{32,48},{40,56},{48,0},{56,8},{64,80... | collective-permute-start | bytes 786440 | tf_op jit(solution)/shard_map/ppermute | solution.py:32
  17.0 12.8 %collective-permute-start.38 = (f32[64,1024]{1,0:T(8,128)S(1)}, f32[64,1024]{1,0:T(8,128)S(1)}, u32[]{:S(2)}, u32[]{:S(2)}) collective-permute-start(f32[64,1024]{1,0:T(8,128)S(1)} %get-tuple-element.145), channel_id=1, source_target_pairs={{0,32},{8,40},{16,48},{24,56},{32,0},{40,8},{48,16},{56,24},{64,96... | collective-permute-start | bytes 786440 | tf_op jit(solution)/shard_map/ppermute | solution.py:32
  17.7 13.9 %collective-permute-start.39 = (f32[64,1024]{1,0:T(8,128)S(1)}, f32[64,1024]{1,0:T(8,128)S(1)}, u32[]{:S(2)}, u32[]{:S(2)}) collective-permute-start(f32[64,1024]{1,0:T(8,128)S(1)} %get-tuple-element.146), channel_id=1, source_target_pairs={{0,48},{8,56},{16,0},{24,8},{32,16},{40,24},{48,32},{56,40},{64,11... | collective-permute-start | bytes 786440 | tf_op jit(solution)/shard_map/ppermute | solution.py:32
  35.2 50.0 %all-to-all-start.5 = ((f32[8,160,512]{2,1,0:T(8,128)}), f32[8,160,512]{2,1,0:T(8,128)S(1)}, u32[]{:S(2)}, u32[]{:S(2)}) async-start(f32[8,160,512]{2,1,0:T(8,128)} %tile.12), calls=%async_computation.5 | async-start | bytes 5242880 | tf_op jit(solution)/shard_map/all_to_all | solution.py:393
  40.9 14.0 %collective-permute-start.43 = (f32[256,1024]{1,0:T(8,128)}, f32[256,1024]{1,0:T(8,128)}, u32[]{:S(2)}, u32[]{:S(2)}) collective-permute-start(f32[256,1024]{1,0:T(8,128)} %copy-done.10), channel_id=1, source_target_pairs={{0,8},{8,0},{1,9},{9,1},{2,10},{10,2},{3,11},{11,3},{4,12},{12,4},... | collective-permute-start | bytes 3145736 | tf_op jit(solution)/shard_map/ppermute | solution.py:37
  44.2 34.4 %collective-permute-start.40 = (f32[16,1024]{1,0:T(8,128)S(1)}, f32[16,1024]{1,0:T(8,128)S(1)}, u32[]{:S(2)}, u32[]{:S(2)}) collective-permute-start(f32[16,1024]{1,0:T(8,128)S(1)} %get-tuple-element.154), channel_id=1, source_target_pairs={{0,64},{8,72},{16,80},{24,88},{32,96},{40,104},{48,112},{56,120},{... | collective-permute-start | bytes 196616 | tf_op jit(solution)/shard_map/ppermute | solution.py:32
  47.5 33.5 %collective-permute-start.41 = (f32[16,1024]{1,0:T(8,128)}, f32[16,1024]{1,0:T(8,128)S(1)}, u32[]{:S(2)}, u32[]{:S(2)}) collective-permute-start(f32[16,1024]{1,0:T(8,128)} %get-tuple-element.155), channel_id=1, source_target_pairs={{0,128},{8,136},{16,144},{24,152},{32,160},{40,168},{48,176},{56,1... | collective-permute-start | bytes 196616 | tf_op jit(solution)/shard_map/ppermute | solution.py:32
  52.1 28.9 %collective-permute-start.42 = (f32[16,1024]{1,0:T(8,128)}, f32[16,1024]{1,0:T(8,128)S(1)}, u32[]{:S(2)}, u32[]{:S(2)}) collective-permute-start(f32[16,1024]{1,0:T(8,128)} %get-tuple-element.156), channel_id=1, source_target_pairs={{0,192},{8,200},{16,208},{24,216},{32,224},{40,232},{48,240},{56,2... | collective-permute-start | bytes 196616 | tf_op jit(solution)/shard_map/ppermute | solution.py:32
  81.0 12.4 %collective-permute-start.47 = (f32[128,1024]{1,0:T(8,128)}, f32[128,1024]{1,0:T(8,128)}, u32[]{:S(2)}, u32[]{:S(2)}) collective-permute-start(f32[128,1024]{1,0:T(8,128)} %get-tuple-element.166), channel_id=1, source_target_pairs={{0,16},{8,24},{1,17},{9,25},{2,18},{10,26},{3,19},{11,27},{4,20},{... | collective-permute-start | bytes 1572872 | tf_op jit(solution)/shard_map/ppermute | solution.py:37
  82.5 22.2 %collective-permute-start.48 = (f32[128,1024]{1,0:T(8,128)}, f32[128,1024]{1,0:T(8,128)}, u32[]{:S(2)}, u32[]{:S(2)}) collective-permute-start(f32[128,1024]{1,0:T(8,128)} %get-tuple-element.167), channel_id=1, source_target_pairs={{0,32},{8,40},{1,33},{9,41},{2,34},{10,42},{3,35},{11,43},{4,36},{... | collective-permute-start | bytes 1572872 | tf_op jit(solution)/shard_map/ppermute | solution.py:37
  83.7 20.9 %collective-permute-start.49 = (f32[128,1024]{1,0:T(8,128)}, f32[128,1024]{1,0:T(8,128)}, u32[]{:S(2)}, u32[]{:S(2)}) collective-permute-start(f32[128,1024]{1,0:T(8,128)} %get-tuple-element.168), channel_id=1, source_target_pairs={{0,48},{8,56},{1,49},{9,57},{2,50},{10,58},{3,51},{11,59},{4,52},{... | collective-permute-start | bytes 1572872 | tf_op jit(solution)/shard_map/ppermute | solution.py:37
  85.9 22.1 %all-to-all-start.6 = ((f32[8,16,256]{2,1,0:T(8,128)}), f32[8,16,256]{2,1,0:T(8,128)}, u32[]{:S(2)}, u32[]{:S(2)}) async-start(f32[8,16,256]{2,1,0:T(8,128)} %tile.13), calls=%async_computation.6 | async-start | bytes 262144 | tf_op jit(solution)/shard_map/all_to_all | solution.py:383
  90.5 18.3 %collective-permute-start.44 = (f32[16,1024]{1,0:T(8,128)S(1)}, f32[16,1024]{1,0:T(8,128)S(1)}, u32[]{:S(2)}, u32[]{:S(2)}) collective-permute-start(f32[16,1024]{1,0:T(8,128)S(1)} %get-tuple-element.162.refs_0_), channel_id=1, source_target_pairs={{0,64},{8,72},{16,80},{24,88},{32,96},{40,104},{48,112},{56,120},{... | collective-permute-start | bytes 196616 | tf_op jit(solution)/shard_map/ppermute | solution.py:32
  92.2 16.6 %collective-permute-start.45 = (f32[16,1024]{1,0:T(8,128)S(1)}, f32[16,1024]{1,0:T(8,128)S(1)}, u32[]{:S(2)}, u32[]{:S(2)}) collective-permute-start(f32[16,1024]{1,0:T(8,128)S(1)} %get-tuple-element.162.refs_0_), channel_id=1, source_target_pairs={{0,128},{8,136},{16,144},{24,152},{32,160},{40,168},{48,176},{56,1... | collective-permute-start | bytes 196616 | tf_op jit(solution)/shard_map/ppermute | solution.py:32
  93.4 15.4 %collective-permute-start.46 = (f32[16,1024]{1,0:T(8,128)S(1)}, f32[16,1024]{1,0:T(8,128)S(1)}, u32[]{:S(2)}, u32[]{:S(2)}) collective-permute-start(f32[16,1024]{1,0:T(8,128)S(1)} %get-tuple-element.162.refs_0_), channel_id=1, source_target_pairs={{0,192},{8,200},{16,208},{24,216},{32,224},{40,232},{48,240},{56,2... | collective-permute-start | bytes 196616 | tf_op jit(solution)/shard_map/ppermute | solution.py:32
  111.2 14.8 %collective-permute-start.53 = (f32[32,1024]{1,0:T(8,128)S(1)}, f32[32,1024]{1,0:T(8,128)S(1)}, u32[]{:S(2)}, u32[]{:S(2)}) collective-permute-start(f32[32,1024]{1,0:T(8,128)S(1)} %get-tuple-element.179), channel_id=1, source_target_pairs={{0,64},{8,72},{16,80},{24,88},{32,96},{40,104},{48,112},{56,120},{... | collective-permute-start | bytes 393224 | tf_op jit(solution)/shard_map/ppermute | solution.py:37
  112.5 13.5 %collective-permute-start.54 = (f32[32,1024]{1,0:T(8,128)}, f32[32,1024]{1,0:T(8,128)S(1)}, u32[]{:S(2)}, u32[]{:S(2)}) collective-permute-start(f32[32,1024]{1,0:T(8,128)} %get-tuple-element.180), channel_id=1, source_target_pairs={{0,128},{8,136},{16,144},{24,152},{32,160},{40,168},{48,176},{56,1... | collective-permute-start | bytes 393224 | tf_op jit(solution)/shard_map/ppermute | solution.py:37
  113.8 12.2 %collective-permute-start.55 = (f32[32,1024]{1,0:T(8,128)}, f32[32,1024]{1,0:T(8,128)S(1)}, u32[]{:S(2)}, u32[]{:S(2)}) collective-permute-start(f32[32,1024]{1,0:T(8,128)} %copy-done.16), channel_id=1, source_target_pairs={{0,192},{8,200},{16,208},{24,216},{32,224},{40,232},{48,240},{56,2... | collective-permute-start | bytes 393224 | tf_op jit(solution)/shard_map/ppermute | solution.py:37
  127.4 17.6 %all-to-all-start.7 = ((f32[8,32,256]{2,1,0:T(8,128)}), f32[8,32,256]{2,1,0:T(8,128)S(1)}, u32[]{:S(2)}, u32[]{:S(2)}) async-start(f32[8,32,256]{2,1,0:T(8,128)} %tile.14), calls=%async_computation.7 | async-start | bytes 524288 | tf_op jit(solution)/shard_map/all_to_all | solution.py:383
  131.7 12.1 %collective-permute-start.57 = (f32[64,1280]{1,0:T(8,128)S(1)}, f32[64,1280]{1,0:T(8,128)}, u32[]{:S(2)}, u32[]{:S(2)}) collective-permute-start(f32[64,1280]{1,0:T(8,128)S(1)} %get-tuple-element.182.refs_0_), channel_id=1, source_target_pairs={{0,32},{8,40},{16,48},{24,56},{32,0},{40,8},{48,16},{56,24},{64,96... | collective-permute-start | bytes 983048 | tf_op jit(solution)/shard_map/ppermute | solution.py:32
  135.2 9.7 %collective-permute-start.58 = (f32[64,1280]{1,0:T(8,128)S(1)}, f32[64,1280]{1,0:T(8,128)}, u32[]{:S(2)}, u32[]{:S(2)}) collective-permute-start(f32[64,1280]{1,0:T(8,128)S(1)} %get-tuple-element.182.refs_0_), channel_id=1, source_target_pairs={{0,48},{8,56},{16,0},{24,8},{32,16},{40,24},{48,32},{56,40},{64,11... | collective-permute-start | bytes 983048 | tf_op jit(solution)/shard_map/ppermute | solution.py:32
  138.5 8.6 %collective-permute-start.59 = (f32[64,1280]{1,0:T(8,128)S(1)}, f32[64,1280]{1,0:T(8,128)}, u32[]{:S(2)}, u32[]{:S(2)}) collective-permute-start(f32[64,1280]{1,0:T(8,128)S(1)} %get-tuple-element.182.refs_0_), channel_id=1, source_target_pairs={{0,8},{8,0},{16,24},{24,16},{32,40},{40,32},{48,56},{56,48},{64,72... | collective-permute-start | bytes 983048 | tf_op jit(solution)/shard_map/ppermute | solution.py:32
  138.9 8.2 %collective-permute-start.60 = (f32[64,1280]{1,0:T(8,128)}, f32[64,1280]{1,0:T(8,128)}, u32[]{:S(2)}, u32[]{:S(2)}) collective-permute-start(f32[64,1280]{1,0:T(8,128)} %collective-permute-done.56.refs_1_), channel_id=1, source_target_pairs={{0,8},{8,0},{16,24},{24,16},{32,40},{40,32},{48,56},{56,48},{64,72... | collective-permute-start | bytes 983048 | tf_op jit(solution)/shard_map/ppermute | solution.py:32
  (18 other events, 88.6 us)
